TPU v7x, 256 devices: a whole 4x4x8 slice. The times are simulated.
256 devices in a mesh: dp: 32 (over z, x), head: 8 (over y, core).
Axes of the slice: x: 4, y: 4, z: 8, core: 2. Of those that a mesh axis runs over, the one named last changes fastest.
Arguments:
- tokens: bfloat16 [32768, 2048], P(('dp', 'head')), may hold values from -8 to 8
- stretch_prompt: int32 [64], replicated, may hold values from 0 to 7, never falling along the last dimension, each value on 1 to 32 neighbouring positions
- last_fill: int32 [64], replicated, may hold values from 1 to 512
- ln1_gain: bfloat16 [2048], replicated, may hold values from 0.25 to 1.75
- w_qk: bfloat16 [2048, 2, 2048], P(None, None, 'head'), may hold values from -0.125 to 0.125
- w_vz: bfloat16 [2048, 2, 4096], P(None, None, 'head'), may hold values from -0.125 to 0.125
- w_ba: bfloat16 [2048, 2, 32], P(None, None, 'head'), may hold values from -2 to 2
- conv_qk: bfloat16 [4, 2, 2048], P(None, None, 'head'), may hold values from -3 to 3
- conv_value: bfloat16 [4, 4096], P(None, 'head'), may hold values from -3 to 3
- decay_log: float32 [32], P('head'), may hold values from 0 to 1
- dt_bias: float32 [32], P('head'), may hold values from -25 to -3
- norm_gain: bfloat16 [128], replicated, may hold values from 0.25 to 1.75
- w_out: bfloat16 [4096, 2048], P('head'), may hold values from -0.09375 to 0.09375
- ln2_gain: bfloat16 [2048], replicated, may hold values from 0.25 to 1.75
- w_sgate: bfloat16 [2048], replicated, may hold values from -0.125 to 0.125
- shared_weights: bfloat16 [3, 512, 2048], P(None, 'head'), may hold values from -0.25 to 0.25
Outputs:
- attention_out: bfloat16 [32768, 2048], P(('dp', 'head'))
- layer_out: bfloat16 [32768, 2048], P(('dp', 'head'))
Inputs may be any that keep to these rules, and one draw needn't show every extreme that they name: stretch_prompt never falls from one stretch to the next, so each prompt holds consecutive stretches; every prompt holds 1 to 32 stretches and one holds exactly 32.
All inputs are finite; a program needn't handle non-finite values.
Results may differ from a plain program's by a relative error of at most 0.025.
Values may be sent and summed in bfloat16 or wider, within the bound.
No kernel may reach another device: no remote copies, remote signals or barrier semaphores. Data moves between devices by JAX's collectives and lax.ppermute only.
A program may use at most 128 MiB of HBM per device.

v0:
```python
import itertools

import jax
import jax.numpy as jnp
from jax import lax
from jax.experimental import pallas as pl
from jax.experimental.pallas import tpu as pltpu
from jax.sharding import Mesh
from jax.sharding import PartitionSpec as P

F32 = jnp.float32
BF16 = jnp.bfloat16
EPSILON = 1e-06
DK = 128
STRETCH = 512
ROWS = 128
CHUNKS = 8
HEADS = 4
KEYS = 2
NZ, NX, NY, NC = 8, 4, 4, 2
LEAD = 16
COL_K = 256
COL_V = 512
COL_BA = 1024
COL_END = 1152
MIB = 1024 * 1024
PLACES = {
    (0, 0): (0, 0),
    (0, 1): (0, 1),
    (1, 0): (1, 0),
    (3, 0): (1, 1),
    (1, 1): (1, 2),
    (3, 1): (1, 3),
    (2, 0): (2, 0),
    (2, 1): (2, 1),
}


def dot(left, right, contract=((1,), (0,))):
    return lax.dot_general(left, right, (contract, ((), ())), preferred_element_type=F32)


def silu(value):
    return value * (0.5 * jnp.tanh(0.5 * value) + 0.5)


def sigmoid(value):
    return 0.5 * jnp.tanh(0.5 * value) + 0.5


def scaled_rows(inputs, scaling):
    widened = inputs.astype(F32)
    spread = jnp.mean(widened * widened, axis=-1, keepdims=True)
    return widened * lax.rsqrt(spread + EPSILON) * scaling.astype(F32)


def hold(value):
    return pltpu.with_memory_space_constraint(value, pltpu.HBM)


def turn(value, axis, steps, count):
    return lax.ppermute(value, axis, [(i, (i + steps) % count) for i in range(count)])


def push(value, axis, steps, count):
    return lax.ppermute(value, axis, [(i, i + steps) for i in range(count - steps)])


def mixed_rows(ref, chunk, first, last, taps, reset):
    start = chunk * ROWS if isinstance(chunk, int) else pl.multiple_of(chunk * ROWS, ROWS)
    rows = ref[pl.ds(start, ROWS + LEAD), first:last].astype(F32)
    if reset is not False:
        rows = jnp.concatenate([jnp.where(reset, 0.0, rows[:LEAD]), rows[LEAD:]], axis=0)
    total = rows[LEAD:] * taps[3:4]
    for offset in (1, 2, 3):
        total = total + rows[LEAD - offset : LEAD - offset + ROWS] * taps[3 - offset : 4 - offset]
    return silu(total)


def unit_heads(value):
    parts = []
    for head in range(value.shape[1] // DK):
        part = value[:, head * DK : (head + 1) * DK]
        parts.append(part * lax.rsqrt(jnp.sum(part * part, axis=-1, keepdims=True) + EPSILON))
    return parts


def fetch_rows(scal, pieces, scratch, sems, first, last, target):
    copies = []
    for (steps, other), (piece, block) in PLACES.items():
        row = lax.rem(scal[0] + steps, NY)
        core = scal[1] if other == 0 else 1 - scal[1]
        chunk = row * NC + core
        start = pl.multiple_of(chunk * ROWS + LEAD, LEAD)
        copy = pltpu.make_async_copy(
            pieces[piece].at[pl.ds(block * ROWS, ROWS), pl.ds(first, last - first)],
            scratch.at[pl.ds(start, ROWS), pl.ds(target, last - first)],
            sems.at[len(copies)],
        )
        copy.start()
        copies.append(copy)
    for copy in copies:
        copy.wait()


def is_reset(scal, chunk):
    if isinstance(chunk, int):
        return scal[2 + chunk * 2 // CHUNKS] > 0 if chunk % (CHUNKS // 2) == 0 else False
    first = jnp.logical_and(chunk == 0, scal[2] > 0)
    second = jnp.logical_and(chunk == CHUNKS // 2, scal[3] > 0)
    return jnp.logical_or(first, second)


def iota2(axis):
    return lax.broadcasted_iota(jnp.int32, (ROWS, ROWS), axis)


def odd_blocks(value, span):
    return jnp.concatenate([value[at : at + span] for at in range(span, ROWS, 2 * span)], axis=0)


def with_even(even, odd, span):
    parts = []
    for place, at in enumerate(range(0, ROWS, 2 * span)):
        block = odd[place * span : (place + 1) * span]
        parts.append(jnp.zeros_like(block) if even is None else even[at : at + span])
        parts.append(block)
    return jnp.concatenate(parts, axis=0)


def inverse_rests(stricts, level):
    rests = [jnp.where(level == 1, -strict, 0.0) for strict in stricts]
    for step in (2, 3):
        lows = [rest.astype(BF16) for rest in rests]
        belows = [jnp.where(level == step, strict, 0.0) for strict in stricts]
        halves = [below + dot(below.astype(BF16), low) for below, low in zip(belows, lows)]
        yield
        rests = [rest - half - dot(low, half.astype(BF16)) for rest, half, low in zip(rests, halves, lows)]
        yield
    for step in (4, 5, 6, 7):
        span = 1 << (step - 1)
        here = odd_blocks(level, span) == step
        lows = [rest.astype(BF16) for rest in rests]
        odds = [odd_blocks(rest, span) for rest in rests]
        belows = [jnp.where(here, odd_blocks(strict, span), 0.0) for strict in stricts]
        halves = [below + dot(below.astype(BF16), low) for below, low in zip(belows, lows)]
        yield
        wides = [with_even(None, half, span).astype(BF16) for half in halves]
        odds = [odd - half - dot(odd.astype(BF16), wide) for odd, half, wide in zip(odds, halves, wides)]
        rests = [with_even(rest, odd, span) for rest, odd in zip(rests, odds)]
        yield
    return rests


def block_levels():
    row, col = iota2(0), iota2(1)
    apart = jnp.where(row > col, jnp.bitwise_xor(row, col), 0)
    level = jnp.zeros((ROWS, ROWS), jnp.int32)
    for step in range(7):
        level = level + (apart >= (1 << step)).astype(jnp.int32)
    return level


def state_kernel(
    scal, piece_a, piece_b, piece_c, tail, taps, decay, bias,
    xend, xs_out, vs_out, khat_out, logs_out,
    raw, rest, kturn, values, betas, state, xs, vs, khat, logs, sems, out_sems,
):
    raw[0:LEAD, 0:COL_BA] = tail[...]
    fetch_rows(scal, (piece_a, piece_b, piece_c), raw, sems, COL_K, COL_END, COL_K)
    row, col = iota2(0), iota2(1)
    strict = row > col
    summing = (row >= col).astype(F32)
    level = block_levels()

    def prepare(chunk):
        reset = is_reset(scal, chunk)
        mixed = mixed_rows(raw, chunk, COL_K, COL_BA, taps, reset)
        start = chunk * ROWS + LEAD
        start = start if isinstance(chunk, int) else pl.multiple_of(start, LEAD)
        ba = raw[pl.ds(start, ROWS), COL_BA:COL_END].astype(F32)
        beta = sigmoid(ba)
        inner = ba + bias[...]
        soft = jnp.maximum(inner, 0.0) + jnp.log1p(jnp.exp(-jnp.abs(inner)))
        rate = -jnp.exp(decay[...]) * soft
        log = lax.dot_general(
            summing, rate, (((1,), (0,)), ((), ())),
            precision=lax.Precision.HIGHEST, preferred_element_type=F32,
        )
        log_turned = log.T
        betas[chunk] = beta
        logs[chunk] = log
        unit = unit_heads(mixed[:, : KEYS * DK])
        lowers = []
        for key in range(KEYS):
            key_rows = unit[key].astype(BF16)
            khat[chunk, key] = key_rows
            kturn[chunk, key] = unit[key].T.astype(BF16)
            products = dot(key_rows, key_rows, ((1,), (1,)))
            for half in range(2):
                head = 2 * key + half
                beta_col = beta[:, head : head + 1]
                spread = log[:, HEADS + head : HEADS + head + 1] - log_turned[HEADS + head : HEADS + head + 1, :]
                weight = jnp.exp(jnp.minimum(spread, 0.0))
                lower = jnp.where(strict, products * beta_col * weight, 0.0)
                lowers.append(lower)
                value = mixed[:, (KEYS + head) * DK : (KEYS + head + 1) * DK]
                values[chunk, head] = value * beta_col
        return lowers

    def prepare_all(chunks):
        lowers = []
        for chunk in chunks:
            lowers += prepare(chunk)
            yield
        found = yield from inverse_rests(lowers, level)
        for place, value in enumerate(found):
            rest[chunks[place // HEADS], place % HEADS] = value.astype(BF16)

    opening = jnp.where(scal[2] > 0, 0.0, 1.0)
    identity = jnp.where(row == col, opening, 0.0)
    for key in range(KEYS):
        for half in range(2):
            state[key, :, 2 * half * DK : (2 * half + 1) * DK] = jnp.zeros((DK, DK), F32)
            state[key, :, (2 * half + 1) * DK : (2 * half + 2) * DK] = identity

    def advance(chunk):
        beta = betas[chunk]
        log = logs[chunk]
        growth = jnp.exp(log)
        last = log[ROWS - 1 : ROWS, :]
        shrink = jnp.exp(last - log)
        whole = jnp.exp(last)
        held = [state[key] for key in range(KEYS)]
        fresh = jnp.logical_and(chunk == CHUNKS // 2, scal[3] > 0)
        held = [jnp.where(fresh, 0.0, value) for value in held]
        lows = [value.astype(BF16) for value in held]
        for key in range(KEYS):
            xs[chunk, key] = lows[key]
        seen = [dot(khat[chunk, key], lows[key]) for key in range(KEYS)]
        yield
        wanted = []
        for head in range(HEADS):
            at = HEADS + head
            half = head % 2
            factor = beta[:, head : head + 1] * growth[:, at : at + 1]
            part = seen[head // 2][:, 2 * half * DK : (2 * half + 2) * DK] * factor
            wanted.append(jnp.concatenate([values[chunk, head] - part[:, :DK], -part[:, DK:]], axis=1))
        solved = [
            value + dot(rest[chunk, head], value.astype(BF16)) for head, value in enumerate(wanted)
        ]
        yield
        updates = []
        scales = []
        for head in range(HEADS):
            at = HEADS + head
            vs[chunk, head] = solved[head].astype(BF16)
            updates.append((solved[head] * shrink[:, at : at + 1]).astype(BF16))
            scales.append(jnp.broadcast_to(whole[:, at : at + 1], (1, 2 * DK)))
        for key in range(KEYS):
            scale = jnp.concatenate(scales[2 * key : 2 * key + 2], axis=1)
            update = jnp.concatenate(updates[2 * key : 2 * key + 2], axis=1)
            state[key] = held[key] * scale + dot(kturn[chunk, key], update)
        for copy in copies_out(chunk):
            copy.start()
        yield

    def advance_all(chunks):
        for chunk in chunks:
            yield from advance(chunk)

    def copies_out(chunk):
        return [
            pltpu.make_async_copy(held.at[chunk], target.at[chunk], out_sems.at[place, chunk])
            for place, (held, target) in enumerate(((xs, xs_out), (vs, vs_out), (khat, khat_out), (logs, logs_out)))
        ]

    def both(pair, unused):
        chain = advance_all((2 * pair - 2, 2 * pair - 1))
        for place, also_unused in enumerate(prepare_all((2 * pair, 2 * pair + 1))):
            if place % 2 == 1:
                next(chain, None)
        for also_unused in chain:
            pass
        return unused

    def last(chunk, unused):
        for also_unused in advance(chunk):
            pass
        return unused

    for unused in prepare_all((0, 1)):
        pass
    lax.fori_loop(1, CHUNKS // 2, both, 0)
    lax.fori_loop(CHUNKS - 2, CHUNKS, last, 0)
    for key in range(KEYS):
        for half in range(2):
            xend[2 * key + half] = state[key, :, 2 * half * DK : (2 * half + 2) * DK].astype(BF16)
    for chunk in range(CHUNKS):
        for copy in copies_out(chunk):
            copy.wait()


def state_call(scal, pieces, tail, taps, decay, bias):
    vmem = pl.BlockSpec(memory_space=pltpu.VMEM)
    hbm = pl.BlockSpec(memory_space=pltpu.HBM)
    return pl.pallas_call(
        state_kernel,
        out_shape=(
            jax.ShapeDtypeStruct((HEADS, DK, 2 * DK), BF16),
            pltpu.HBM((CHUNKS, KEYS, DK, 4 * DK), BF16),
            pltpu.HBM((CHUNKS, HEADS, ROWS, 2 * DK), BF16),
            pltpu.HBM((CHUNKS, KEYS, ROWS, DK), BF16),
            pltpu.HBM((CHUNKS, ROWS, 128), F32),
        ),
        in_specs=[pl.BlockSpec(memory_space=pltpu.SMEM), hbm, hbm, hbm] + [vmem] * 4,
        out_specs=[vmem] + [hbm] * 4,
        scratch_shapes=[
            pltpu.VMEM((LEAD + CHUNKS * ROWS, COL_END), BF16),
            pltpu.VMEM((CHUNKS, HEADS, ROWS, ROWS), BF16),
            pltpu.VMEM((CHUNKS, KEYS, DK, ROWS), BF16),
            pltpu.VMEM((CHUNKS, HEADS, ROWS, DK), F32),
            pltpu.VMEM((CHUNKS, ROWS, 128), F32),
            pltpu.VMEM((KEYS, DK, 4 * DK), F32),
            pltpu.VMEM((CHUNKS, KEYS, DK, 4 * DK), BF16),
            pltpu.VMEM((CHUNKS, HEADS, ROWS, 2 * DK), BF16),
            pltpu.VMEM((CHUNKS, KEYS, ROWS, DK), BF16),
            pltpu.VMEM((CHUNKS, ROWS, 128), F32),
            pltpu.SemaphoreType.DMA((CHUNKS,)),
            pltpu.SemaphoreType.DMA((4, CHUNKS)),
        ],
        compiler_params=pltpu.CompilerParams(vmem_limit_bytes=40 * MIB),
        cost_estimate=pl.CostEstimate(flops=6_000_000_000, bytes_accessed=20_000_000, transcendentals=0),
        name="state",
    )(scal, *map(hold, pieces), tail, taps, decay, bias)


def read_kernel(
    scal, piece_a, piece_b, piece_c, tail, taps, xs, vs, khat, logs, out, raw, sems
):
    step = pl.program_id(0)

    @pl.when(step == 0)
    def _():
        raw[0:LEAD, :] = tail[...]
        fetch_rows(scal, (piece_a, piece_b, piece_c), raw, sems, 0, COL_K, 0)

    inclusive = iota2(0) >= iota2(1)
    queries, weights, growths = [], [], []
    for core in range(NC):
        chunk = NC * step + core
        start = pl.multiple_of(chunk * ROWS, ROWS)
        reset = is_reset(scal, chunk) if core == 0 else False
        mixed = mixed_rows(raw.at[pl.ds(start, ROWS + LEAD)], 0, 0, COL_K, taps, reset)
        queries += [(value * DK ** (-0.5)).astype(BF16) for value in unit_heads(mixed)]
        log = logs[core]
        log_turned = log.T
        growth = jnp.exp(log)
        for head in range(HEADS):
            at = HEADS + head
            growths.append(growth[:, at : at + 1])
            spread = log[:, at : at + 1] - log_turned[at : at + 1, :]
            weights.append(jnp.where(inclusive, jnp.exp(jnp.minimum(spread, 0.0)), 0.0))
    pairs = [(core, key) for core in range(NC) for key in range(KEYS)]
    products = [dot(queries[i], khat[core, key], ((1,), (1,))) for i, (core, key) in enumerate(pairs)]
    seen = [dot(queries[i], xs[core, key]) for i, (core, key) in enumerate(pairs)]
    for core in range(NC):
        other = jnp.bitwise_xor(core, scal[1])
        for head in range(HEADS):
            pair = core * KEYS + head // 2
            half = head % 2
            scores = (products[pair] * weights[core * HEADS + head]).astype(BF16)
            found = seen[pair][:, 2 * half * DK : (2 * half + 2) * DK] * growths[core * HEADS + head]
            out[other, head] = (found + dot(scores, vs[core, head])).astype(BF16)


def read_call(scal, pieces, tail, taps, xs, vs, khat, logs):
    hbm = pl.BlockSpec(memory_space=pltpu.HBM)
    return pl.pallas_call(
        read_kernel,
        out_shape=pltpu.HBM((NC, NY, HEADS, ROWS, 2 * DK), BF16),
        grid_spec=pltpu.PrefetchScalarGridSpec(
            num_scalar_prefetch=1,
            grid=(CHUNKS // NC,),
            in_specs=[
                hbm,
                hbm,
                hbm,
                pl.BlockSpec((LEAD, COL_K), lambda c, scal: (0, 0)),
                pl.BlockSpec((4, COL_K), lambda c, scal: (0, 0)),
                pl.BlockSpec((NC, KEYS, DK, 4 * DK), lambda c, scal: (c, 0, 0, 0)),
                pl.BlockSpec((NC, HEADS, ROWS, 2 * DK), lambda c, scal: (c, 0, 0, 0)),
                pl.BlockSpec((NC, KEYS, ROWS, DK), lambda c, scal: (c, 0, 0, 0)),
                pl.BlockSpec((NC, ROWS, 128), lambda c, scal: (c, 0, 0)),
            ],
            out_specs=pl.BlockSpec(
                (NC, None, HEADS, ROWS, 2 * DK),
                lambda c, scal: (0, lax.rem(c - scal[0] + NY, NY), 0, 0, 0),
            ),
            scratch_shapes=[
                pltpu.VMEM((LEAD + CHUNKS * ROWS, COL_K), BF16),
                pltpu.SemaphoreType.DMA((CHUNKS,)),
            ],
        ),
        compiler_params=pltpu.CompilerParams(vmem_limit_bytes=32 * MIB),
        cost_estimate=pl.CostEstimate(flops=3_000_000_000, bytes_accessed=10_000_000, transcendentals=0),
        name="read",
    )(scal, *map(hold, pieces), tail, taps, hold(xs), hold(vs), hold(khat), hold(logs))


def norm_kernel(tokens, gain, out):
    out[...] = scaled_rows(tokens[...], gain[...][None, :]).astype(BF16)


def norm_call(tokens, gain):
    vmem = pl.BlockSpec(memory_space=pltpu.VMEM)
    return pl.pallas_call(
        norm_kernel,
        out_shape=jax.ShapeDtypeStruct(tokens.shape, BF16),
        in_specs=[vmem, vmem],
        out_specs=vmem,
        cost_estimate=pl.CostEstimate(flops=1_000_000, bytes_accessed=1_000_000, transcendentals=0),
        name="norm",
    )(tokens, gain)


def after(late, early):
    moved = dot(late[:, DK:], early)
    if early.shape[1] == DK:
        return moved + late[:, :DK].astype(F32)
    return jnp.concatenate([moved[:, :DK] + late[:, :DK].astype(F32), moved[:, DK:]], axis=1)


def row_kernel(parts, leads, whole, sums):
    held = parts[0]
    leads[0] = held
    for place in range(1, NX):
        held = after(parts[place], held).astype(BF16)
        if place < NX - 1:
            leads[place] = held
    whole[...] = held
    sums[...] = held[:, :DK]


def row_call(parts):
    vmem = pl.BlockSpec(memory_space=pltpu.VMEM)
    return pl.pallas_call(
        row_kernel,
        out_shape=(
            jax.ShapeDtypeStruct((NX - 1, DK, 2 * DK), BF16),
            jax.ShapeDtypeStruct((DK, 2 * DK), BF16),
            jax.ShapeDtypeStruct((DK, DK), BF16),
        ),
        in_specs=[vmem],
        out_specs=[vmem] * 3,
        cost_estimate=pl.CostEstimate(flops=100_000_000, bytes_accessed=1_000_000, transcendentals=0),
        name="rows",
    )(parts)


def open_kernel(one, two, three, four, leads, out):
    opening = four[...]
    for earlier in (three, two, one):
        opening = after(earlier[...], opening).astype(BF16)
    out[0] = opening
    for place in range(1, NX):
        out[place] = after(leads[place - 1], opening).astype(BF16)


def open_call(earlier, leads):
    vmem = pl.BlockSpec(memory_space=pltpu.VMEM)
    return pl.pallas_call(
        open_kernel,
        out_shape=jax.ShapeDtypeStruct((NX, DK, DK), BF16),
        in_specs=[vmem] * 5,
        out_specs=vmem,
        cost_estimate=pl.CostEstimate(flops=100_000_000, bytes_accessed=1_000_000, transcendentals=0),
        name="open",
    )(*earlier, leads)


def out_kernel(other, scal, found, gates, opening, gain, w_out, out):
    rows = []
    moved = [
        [dot(found[block, head][:, DK:], opening[head]) for head in range(HEADS)]
        for block in range(2)
    ]
    for block in range(2):
        steps = 2 * pl.program_id(0) + block
        core = scal[1] if other == 0 else 1 - scal[1]
        chunk = lax.rem(scal[0] + steps, NY) * NC + core
        first = lax.rem(chunk, STRETCH // ROWS) * ROWS
        fill = jnp.where(chunk < CHUNKS // 2, scal[4], scal[5])
        within = lax.broadcasted_iota(jnp.int32, (ROWS, 1), 0) + first
        kept = within < fill
        parts = []
        for head in range(HEADS):
            value = found[block, head][:, :DK].astype(F32) + moved[block][head]
            value = jnp.where(kept, value, 0.0)
            gate = gates[block, :, head * DK : (head + 1) * DK].astype(F32)
            spread = jnp.mean(value * value, axis=-1, keepdims=True)
            parts.append((value * lax.rsqrt(spread + EPSILON) * gain[...] * silu(gate)).astype(BF16))
        rows.append(jnp.concatenate(parts, axis=1))
    total = dot(jnp.concatenate(rows, axis=0), w_out[...]).astype(BF16)
    out[...] = total.reshape(out.shape)


def out_call(other, scal, found, gates, opening, gain, w_out):
    width = w_out.shape[1]
    return pl.pallas_call(
        lambda *refs: out_kernel(other, *refs),
        grid=(NY // 2,),
        out_shape=jax.ShapeDtypeStruct((NY, ROWS, width), BF16),
        in_specs=[
            pl.BlockSpec(memory_space=pltpu.SMEM),
            pl.BlockSpec((None, 2, HEADS, ROWS, 2 * DK), lambda i: (other, i, 0, 0, 0)),
            pl.BlockSpec((2, ROWS, HEADS * DK), lambda i: (i, 0, 0)),
            pl.BlockSpec((HEADS, DK, DK), lambda i: (0, 0, 0)),
            pl.BlockSpec((1, DK), lambda i: (0, 0)),
            pl.BlockSpec((HEADS * DK, width), lambda i: (0, 0)),
        ],
        out_specs=pl.BlockSpec((2, ROWS, width), lambda i: (i, 0, 0)),
        compiler_params=pltpu.CompilerParams(vmem_limit_bytes=32 * MIB),
        cost_estimate=pl.CostEstimate(flops=1_200_000_000, bytes_accessed=6_000_000, transcendentals=0),
        name="out",
    )(scal, hold(found), hold(gates), opening, gain, w_out)


def sum_kernel(own, received, rows, pass_up, pass_down, free_up, free_down, more_up, more_down):
    half = own.shape[2] // 2
    total = own[2].astype(F32) + received[2].astype(F32)
    pass_up[...] = total[:, :half].astype(BF16)
    pass_down[...] = total[:, half:].astype(BF16)
    total = own[1].astype(F32) + received[1].astype(F32)
    more_up[...] = total[:, :half].astype(BF16)
    free_up[...] = total[:, half:].astype(BF16)
    total = own[3].astype(F32) + received[3].astype(F32)
    free_down[...] = total[:, :half].astype(BF16)
    more_down[...] = total[:, half:].astype(BF16)
    rows[...] = (own[0].astype(F32) + received[0].astype(F32)).astype(BF16)


def sum_call(own, received):
    vmem = pl.BlockSpec(memory_space=pltpu.VMEM)
    width = own.shape[2]
    half = jax.ShapeDtypeStruct((ROWS, width // 2), BF16)
    return pl.pallas_call(
        sum_kernel,
        out_shape=(jax.ShapeDtypeStruct((ROWS, width), BF16),) + (half,) * 6,
        in_specs=[vmem] * 2,
        out_specs=[vmem] * 7,
        compiler_params=pltpu.CompilerParams(vmem_limit_bytes=16 * MIB),
        cost_estimate=pl.CostEstimate(flops=1_000_000, bytes_accessed=6_000_000, transcendentals=0),
        name="sum",
    )(own, received)


def expert_kernel(
    rows, more_up, free_up, free_down, more_down, tokens, gain, w_sgate, shared,
    attention, layer, weights, sems,
):
    size = shared.shape[1] // 4
    copies = [
        [
            pltpu.make_async_copy(
                shared.at[place, pl.ds(part * size, size)],
                weights.at[place, pl.ds(part * size, size)],
                sems.at[4 * place + part],
            )
            for part in range(4)
        ]
        for place in range(3)
    ]
    for place in range(3):
        for copy in copies[place]:
            copy.start()
    ups = jnp.concatenate([more_up[...], free_up[...]], axis=1)
    downs = jnp.concatenate([free_down[...], more_down[...]], axis=1)
    total = rows[...].astype(F32) + ups.astype(F32) + downs.astype(F32)
    total = total.astype(BF16)
    attention[...] = total
    residual = (tokens[...].astype(F32) + total.astype(F32)).astype(BF16)
    normed = scaled_rows(residual, gain[...][None, :]).astype(BF16)
    weighed = normed.astype(F32) * w_sgate[...][None, :].astype(F32)
    gate = sigmoid(jnp.sum(weighed, axis=-1, keepdims=True))
    for copy in copies[0]:
        copy.wait()
    gate_part = dot(normed, weights[0], ((1,), (1,)))
    for copy in copies[1]:
        copy.wait()
    up_part = dot(normed, weights[1], ((1,), (1,)))
    hidden = (silu(gate_part) * up_part).astype(BF16)
    for copy in copies[2]:
        copy.wait()
    layer[...] = (residual.astype(F32) + gate * dot(hidden, weights[2])).astype(BF16)


def expert_call(rows, more_up, free_up, free_down, more_down, tokens, gain, w_sgate, shared):
    vmem = pl.BlockSpec(memory_space=pltpu.VMEM)
    return pl.pallas_call(
        expert_kernel,
        out_shape=(jax.ShapeDtypeStruct(tokens.shape, BF16),) * 2,
        in_specs=[vmem] * 8 + [pl.BlockSpec(memory_space=pltpu.HBM)],
        out_specs=[vmem] * 2,
        scratch_shapes=[pltpu.VMEM(shared.shape, BF16), pltpu.SemaphoreType.DMA((12,))],
        compiler_params=pltpu.CompilerParams(vmem_limit_bytes=32 * MIB),
        cost_estimate=pl.CostEstimate(flops=800_000_000, bytes_accessed=9_000_000, transcendentals=0),
        name="expert",
    )(rows, more_up, free_up, free_down, more_down, tokens, gain, w_sgate, hold(shared))


def per_device(
    tokens,
    stretch_prompt,
    last_fill,
    ln1_gain,
    w_qk,
    w_vz,
    w_ba,
    conv_qk,
    conv_value,
    decay_log,
    dt_bias,
    norm_gain,
    w_out,
    ln2_gain,
    w_sgate,
    shared_weights,
):
    width = tokens.shape[1]
    place_y = lax.axis_index("y")
    place_core = lax.axis_index("core")
    device = lax.axis_index("z") * NX + lax.axis_index("x")
    normed = norm_call(tokens, ln1_gain)

    below = turn(normed, "y", 1, NY)
    above = turn(normed, "y", -1, NY)
    beside = turn(normed, "core", 1, NC)
    flat_vz = w_vz.reshape(width, -1)
    half_vz = flat_vz.shape[1] // 2
    weight = jnp.concatenate(
        [
            w_qk.reshape(width, -1),
            flat_vz[:, :half_vz],
            jnp.pad(w_ba.reshape(width, -1), ((0, 0), (0, 128 - 2 * HEADS))),
        ],
        axis=1,
    )
    weight_z = flat_vz[:, half_vz:]

    def project(weight, *parts):
        rows = jnp.concatenate(parts, axis=0)
        return jnp.dot(rows, weight, preferred_element_type=F32).astype(BF16)

    piece_a = project(weight, normed, beside)
    below, above, piece_a = lax.optimization_barrier((below, above, piece_a))
    across_up = turn(below[: ROWS // 2], "y", 1, NY)
    across_down = turn(above[ROWS // 2 :], "y", -1, NY)
    above_beside = turn(above, "core", 1, NC)
    below_beside = turn(below, "core", 1, NC)
    above, below, above_beside, below_beside = lax.optimization_barrier(
        (above, below, above_beside, below_beside)
    )
    piece_b = project(weight, above, below, above_beside, below_beside)
    across_up, across_down, piece_b = lax.optimization_barrier((across_up, across_down, piece_b))
    across = jnp.concatenate([across_up, across_down], axis=0)
    across_beside = turn(across, "core", 1, NC)
    piece_c = project(weight, across, across_beside)
    shared_weights, piece_c = lax.optimization_barrier((shared_weights, piece_c))
    pieces = (piece_a, piece_b, piece_c)
    gathered = lax.all_gather(shared_weights, ("y", "core"), axis=1, tiled=True)

    first_slot = device * 2
    before = jnp.concatenate([jnp.full((1,), -1, jnp.int32), stretch_prompt])
    later = jnp.concatenate([stretch_prompt, jnp.full((1,), -1, jnp.int32)])
    current = lax.dynamic_slice_in_dim(stretch_prompt, first_slot, 2)
    starts = current != lax.dynamic_slice_in_dim(before, first_slot, 2)
    finishes = current != lax.dynamic_slice_in_dim(later, first_slot + 1, 2)
    fill = jnp.where(finishes, lax.dynamic_slice_in_dim(last_fill, first_slot, 2), STRETCH)
    scal = jnp.concatenate(
        [jnp.stack([place_y, place_core]).astype(jnp.int32), starts.astype(jnp.int32), fill]
    )

    last_place = (NY - 1 - place_y) * NC + (NC - 1 - place_core)
    ends = piece_a[ROWS - LEAD : ROWS, :COL_BA]
    for (steps, other), (piece, block) in PLACES.items():
        rows = pieces[piece][(block + 1) * ROWS - LEAD : (block + 1) * ROWS, :COL_BA]
        ends = jnp.where(last_place == steps * NC + other, rows, ends)
    tail = push(ends, ("z", "x"), 1, NZ * NX)

    def gates(*parts):
        rows = jnp.concatenate(parts, axis=0)
        gate = jnp.dot(rows, weight_z, preferred_element_type=F32).astype(BF16)
        return gate.reshape(NY, ROWS, -1)

    gates_beside = gates(beside, above_beside, across_beside, below_beside)
    gates_own = gates(normed, above, across, below)
    tail, gates_own = lax.optimization_barrier((tail, gates_own))
    taps_qk = conv_qk.astype(F32)
    taps_kv = jnp.concatenate([taps_qk[:, 1, :], conv_value.astype(F32)], axis=1)
    pad = ((HEADS, 128 - 2 * HEADS),)
    decay = jnp.pad(decay_log, pad)[None, :]
    bias = jnp.pad(dt_bias, pad)[None, :]
    xend, xs, vs, khat, logs = state_call(scal, pieces, tail, taps_kv, decay, bias)

    parts = lax.all_to_all(xend, "x", 0, 0, tiled=True)
    given = (tail[:, :COL_K], taps_qk[:, 0, :], xs, vs, khat, logs)
    parts, gates_beside = lax.optimization_barrier((parts, gates_beside))
    leads, whole, sums = row_call(parts)
    earlier = [push(whole if steps < 4 else sums, "z", steps, NZ) for steps in (1, 2, 3, 4)]
    openings = open_call(earlier, leads)
    opening = lax.all_to_all(openings, "x", 0, 0, tiled=True)

    found = read_call(scal, pieces, *given)

    gain = norm_gain.astype(F32)[None, :]
    lent = out_call(1, scal, found, gates_beside, opening, gain, w_out)
    received = turn(lent, "core", 1, NC)
    own = out_call(0, scal, found, gates_own, opening, gain, w_out)

    own_rows, pass_up, pass_down, free_up, free_down, more_up, more_down = sum_call(own, received)
    pass_up = turn(pass_up, "y", 1, NY)
    pass_down = turn(pass_down, "y", -1, NY)
    free_up = turn(free_up, "y", 1, NY)
    free_down = turn(free_down, "y", -1, NY)
    more_up = turn((more_up.astype(F32) + pass_up.astype(F32)).astype(BF16), "y", 1, NY)
    more_down = turn((more_down.astype(F32) + pass_down.astype(F32)).astype(BF16), "y", -1, NY)
    return expert_call(
        own_rows, more_up, free_up, free_down, more_down, tokens, ln2_gain, w_sgate, gathered
    )


def solution(mesh):
    fine = Mesh(mesh.devices.reshape(NZ, NX, NY, NC), ("z", "x", "y", "core"))
    rows = P(("z", "x", "y", "core"), None)
    head = ("y", "core")
    return jax.shard_map(
        per_device,
        mesh=fine,
        in_specs=(
            rows,
            P(),
            P(),
            P(),
            P(None, None, head),
            P(None, None, head),
            P(None, None, head),
            P(None, None, head),
            P(None, head),
            P(head),
            P(head),
            P(),
            P(head, None),
            P(),
            P(),
            P(None, head, None),
        ),
        out_specs=(rows, rows),
        check_vma=False,
    )
```

profile of v0, /device:TPU:1, one launch (start us, length us, event | category | flops | bytes accessed | tf_op | source)
XLA Modules:
  0.0 155.0 jit_solution(16168179912631576162)
XLA Ops:
  9.3 3.2 %collective-permute-start.2 = (bf16[128,2048]{1,0:T(8,128)(2,1)}, bf16[128,2048]{1,0:T(8,128)(2,1)S(1)}, u32[]{:S(2)}, u32[]{:S(2)}) collective-permute-start(bf16[128,2048]{1,0:T(8,128)(2,1)} %norm.1), channel_id=1, source_target_pairs={{0,1},{1,0},{2,3},{3,2},{4,5},{5,4},{6,7},{7,6},{8,9},{9,8},{10,11... | collective-permute-start | bytes 1572872 | tf_op jit(solution)/shard_map/ppermute | solution.py:62
  12.5 2.7 %collective-permute-start.1 = (bf16[128,2048]{1,0:T(8,128)(2,1)}, bf16[128,2048]{1,0:T(8,128)(2,1)S(1)}, u32[]{:S(2)}, u32[]{:S(2)}) collective-permute-start(bf16[128,2048]{1,0:T(8,128)(2,1)} %norm.1), channel_id=1, source_target_pairs={{0,6},{2,0},{4,2},{6,4},{1,7},{3,1},{5,3},{7,5},{8,14},{10,8},{12,... | collective-permute-start | bytes 1572872 | tf_op jit(solution)/shard_map/ppermute | solution.py:62
  16.2 3.4 %copy.22 = bf16[256,8,2,512]{3,1,2,0:T(8,128)(2,1)S(1)} copy(bf16[256,8,2,512]{3,2,1,0:T(2,128)(2,1)} %bitcast.25) | data formatting | bytes 8388608
  28.4 2.8 %collective-permute-start.4 = (bf16[64,2048]{1,0:T(8,128)(2,1)S(1)}, bf16[64,2048]{1,0:T(8,128)(2,1)S(1)}, u32[]{:S(2)}, u32[]{:S(2)}) collective-permute-start(bf16[64,2048]{1,0:T(8,128)(2,1)S(1)} %slice.48), channel_id=1, source_target_pairs={{0,6},{2,0},{4,2},{6,4},{1,7},{3,1},{5,3},{7,5},{8,14},{10,8},{12,... | collective-permute-start | bytes 786440 | tf_op jit(solution)/shard_map/ppermute | solution.py:62
  31.2 3.9 %convolution_convert_fusion.piece_b = bf16[512,1152]{1,0:T(8,128)(2,1)} fusion(bf16[128,2048]{1,0:T(8,128)(2,1)S(1)} %collective-permute-done.6, bf16[128,2048]{1,0:T(8,128)(2,1)S(1)} %collective-permute-done.5, bf16[128,2048]{1,0:T(8,128)(2,1)S(1)} %collective-permute-done, bf16[128,2048]{1,0:T(8,128)(2,1)S(1)} %collective-permute-done.1, ...), kind=kOutput, calls=%fused_computation.3 | convolution fusion | flops 2443771904 | bytes 7503872 | tf_op jit(solution)/shard_map/dot_general | solution.py:653
  41.1 2.3 %convolution_convert_fusion.1.piece_c = bf16[256,1152]{1,0:T(8,128)(2,1)} fusion(bf16[128,2048]{1,0:T(8,128)(2,1)S(1)} %collective-permute-done.7, bf16[64,2048]{1,0:T(8,128)(2,1)S(1)} %collective-permute-done.4, bf16[64,2048]{1,0:T(8,128)(2,1)S(1)} %collective-permute-done.3, bf16[2048,8]{1,0:T(8,128)(2,1)S(1)} %copy.20, bf16[2048,512]{1,0:T(8,128)(2,1)S(1)} %slice.61, ...), kind=kOutput, calls=%fused_computation.6 | convolution fusion | flops 1230274560 | bytes 5865472 | tf_op jit(solution)/shard_map/dot_general | solution.py:653
  49.0 16.7 %state.1 = (bf16[4,128,256]{2,1,0:T(8,128)(2,1)}, bf16[8,2,128,512]{3,2,1,0:T(8,128)(2,1)}, bf16[8,4,128,256]{3,2,1,0:T(8,128)(2,1)}, bf16[8,2,128,128]{3,2,1,0:T(8,128)(2,1)}, f32[8,128,128]{2,1,0:T(8,128)}) custom-call(s32[6]{0:T(128)S(1)} %pad_add_fusion.2.scal.refs_0_, bf16[256,1152]{1,0:T(8,128)(2,1)} %copy-done.13, ...), custom_call_target="tpu_custom_call" | custom-call | flops 6000000000 | bytes 20000000 | tf_op jit(solution)/shard_map/state/pallas_call | solution.py:307
  65.7 4.1 %all-to-all-start = ((bf16[4,128,256]{2,1,0:T(8,128)(2,1)}), bf16[4,128,256]{2,1,0:T(8,128)(2,1)S(1)}, u32[]{:S(2)}, u32[]{:S(2)}) async-start(bf16[4,128,256]{2,1,0:T(8,128)(2,1)} %get-tuple-element.50), calls=%async_computation | async-start | bytes 524288 | tf_op jit(solution)/shard_map/all_to_all | solution.py:706
  69.9 3.7 %fusion.19 = bf16[512,512]{1,0:T(8,128)(2,1)} fusion(bf16[2048,1024]{1,0:T(8,128)(2,1)} %bitcast.23, bf16[128,2048]{1,0:T(8,128)(2,1)S(1)} %copy-done.25, bf16[128,2048]{1,0:T(8,128)(2,1)S(1)} %copy-done.27, bf16[128,2048]{1,0:T(8,128)(2,1)S(1)} %copy-done.23, bf16[128,2048]{1,0:T(8,128)(2,1)S(1)} %copy-done.21), kind=kOutput, calls=%fused_computation.23 | convolution fusion | flops 1082392576 | bytes 4718592 | tf_op jit(solution)/shard_map/dot_general | solution.py:693
  78.2 4.3 %collective-permute-start.9 = (bf16[128,256]{1,0:T(8,128)(2,1)}, bf16[128,256]{1,0:T(8,128)(2,1)S(1)}, u32[]{:S(2)}, u32[]{:S(2)}) collective-permute-start(bf16[128,256]{1,0:T(8,128)(2,1)} %get-tuple-element.52), channel_id=1, source_target_pairs={{0,32},{32,64},{64,96},{96,128},{128,160},{160,192},{192,224},{1,3... | collective-permute-start | bytes 196616 | tf_op jit(solution)/shard_map/ppermute | solution.py:66
  82.5 5.3 %collective-permute-start.10 = (bf16[128,256]{1,0:T(8,128)(2,1)}, bf16[128,256]{1,0:T(8,128)(2,1)S(1)}, u32[]{:S(2)}, u32[]{:S(2)}) collective-permute-start(bf16[128,256]{1,0:T(8,128)(2,1)} %get-tuple-element.52), channel_id=1, source_target_pairs={{0,64},{32,96},{64,128},{96,160},{128,192},{160,224},{1,65},{33,97... | collective-permute-start | bytes 196616 | tf_op jit(solution)/shard_map/ppermute | solution.py:66
  87.8 5.3 %collective-permute-start.11 = (bf16[128,256]{1,0:T(8,128)(2,1)}, bf16[128,256]{1,0:T(8,128)(2,1)S(1)}, u32[]{:S(2)}, u32[]{:S(2)}) collective-permute-start(bf16[128,256]{1,0:T(8,128)(2,1)} %get-tuple-element.52), channel_id=1, source_target_pairs={{0,96},{32,128},{64,160},{96,192},{128,224},{1,97},{33,129},{65,16... | collective-permute-start | bytes 196616 | tf_op jit(solution)/shard_map/ppermute | solution.py:66
  93.1 2.3 %collective-permute-start.12 = (bf16[128,128]{1,0:T(8,128)(2,1)}, bf16[128,128]{1,0:T(8,128)(2,1)S(1)}, u32[]{:S(2)}, u32[]{:S(2)}) collective-permute-start(bf16[128,128]{1,0:T(8,128)(2,1)} %get-tuple-element.53), channel_id=1, source_target_pairs={{0,128},{32,160},{64,192},{96,224},{1,129},{33,161},{65,193},{97,2... | collective-permute-start | bytes 98312 | tf_op jit(solution)/shard_map/ppermute | solution.py:66
  99.8 3.3 %all-to-all-start.1 = ((bf16[4,128,128]{2,1,0:T(8,128)(2,1)}), bf16[4,128,128]{2,1,0:T(8,128)(2,1)S(1)}, u32[]{:S(2)}, u32[]{:S(2)}) async-start(bf16[4,128,128]{2,1,0:T(8,128)(2,1)} %open.1), calls=%async_computation.1 | async-start | bytes 262144 | tf_op jit(solution)/shard_map/all_to_all | solution.py:712
  103.1 7.9 %read.1.refs_1_ = bf16[2,4,4,128,256]{4,3,2,1,0:T(8,128)(2,1)} custom-call(s32[6]{0:T(128)S(1)} %pad_add_fusion.2.scal.refs_0_, bf16[256,1152]{1,0:T(8,128)(2,1)} %copy-done.13, bf16[512,1152]{1,0:T(8,128)(2,1)} %convolution_convert_fusion.piece_b, bf16[256,1152]{1,0:T(8,128)(2,1)} %convolution_convert_fusion.1.piece_c, bf16[16,256]{1,0:T(8,128)(2,1)S(1)} %slice.58.tail, ...), custom_call_target="tpu_custom_call" | custom-call | flops 3000000000 | bytes 10000000 | tf_op jit(solution)/shard_map/read/pallas_call | solution.py:379
  111.0 3.3 %out.3 = bf16[4,128,2048]{2,1,0:T(8,128)(2,1)S(1)} custom-call(s32[6]{0:T(128)S(1)} %pad_add_fusion.2.scal.refs_0_, bf16[2,4,4,128,256]{4,3,2,1,0:T(8,128)(2,1)} %read.1.refs_1_, bf16[4,128,512]{2,1,0:T(8,128)(2,1)} %bitcast.31, bf16[4,128,128]{2,1,0:T(8,128)(2,1)S(1)} %all-to-all-done.1.refs_3_, f32[1,128]{1,0:T(1,128)S(1)} %bitcast_convert_fusion.refs_4_, ...), custom_call_target="tpu_custom_call" | custom-call | flops 1200000000 | bytes 6000000 | tf_op jit(solution)/shard_map/out/pallas_call | solution.py:510
  114.3 4.5 %collective-permute-start.13 = (bf16[4,128,2048]{2,1,0:T(8,128)(2,1)S(1)}, bf16[4,128,2048]{2,1,0:T(8,128)(2,1)S(1)}, u32[]{:S(2)}, u32[]{:S(2)}) collective-permute-start(bf16[4,128,2048]{2,1,0:T(8,128)(2,1)S(1)} %out.3), channel_id=1, source_target_pairs={{0,1},{1,0},{2,3},{3,2},{4,5},{5,4},{6,7},{7,6},{8,9},{9,8},{10,11... | collective-permute-start | bytes 6291464 | tf_op jit(solution)/shard_map/ppermute | solution.py:62
  118.8 3.3 %out.2.own = bf16[4,128,2048]{2,1,0:T(8,128)(2,1)S(1)} custom-call(s32[6]{0:T(128)S(1)} %pad_add_fusion.2.scal.refs_0_, bf16[2,4,4,128,256]{4,3,2,1,0:T(8,128)(2,1)} %read.1.refs_1_, bf16[4,128,512]{2,1,0:T(8,128)(2,1)} %bitcast.30, bf16[4,128,128]{2,1,0:T(8,128)(2,1)S(1)} %all-to-all-done.1.refs_3_, f32[1,128]{1,0:T(1,128)S(1)} %bitcast_convert_fusion.refs_4_, ...), custom_call_target="tpu_custom_call" | custom-call | flops 1200000000 | bytes 6000000 | tf_op jit(solution)/shard_map/out/pallas_call | solution.py:510
  125.9 2.7 %collective-permute-start.17 = (bf16[128,1024]{1,0:T(8,128)(2,1)S(1)}, bf16[128,1024]{1,0:T(8,128)(2,1)S(1)}, u32[]{:S(2)}, u32[]{:S(2)}) collective-permute-start(bf16[128,1024]{1,0:T(8,128)(2,1)S(1)} %get-tuple-element.60), channel_id=1, source_target_pairs={{0,6},{2,0},{4,2},{6,4},{1,7},{3,1},{5,3},{7,5},{8,14},{10,8},{12,... | collective-permute-start | bytes 786440 | tf_op jit(solution)/shard_map/ppermute | solution.py:62
  128.6 3.3 %collective-permute-done.14 = bf16[128,1024]{1,0:T(8,128)(2,1)S(1)} collective-permute-done((bf16[128,1024]{1,0:T(8,128)(2,1)S(1)}, bf16[128,1024]{1,0:T(8,128)(2,1)S(1)}, u32[]{:S(2)}, u32[]{:S(2)}) %collective-permute-start.14) | collective-permute-done | bytes 262176 | tf_op jit(solution)/shard_map/ppermute | solution.py:62
  132.2 2.7 %collective-permute-start.19 = (bf16[128,1024]{1,0:T(8,128)(2,1)S(1)}, bf16[128,1024]{1,0:T(8,128)(2,1)S(1)}, u32[]{:S(2)}, u32[]{:S(2)}) collective-permute-start(bf16[128,1024]{1,0:T(8,128)(2,1)S(1)} %add_convert_fusion), channel_id=1, source_target_pairs={{0,6},{2,0},{4,2},{6,4},{1,7},{3,1},{5,3},{7,5},{8,14},{10,8},{12,... | collective-permute-start | bytes 786440 | tf_op jit(solution)/shard_map/ppermute | solution.py:62
  134.9 2.6 %collective-permute-done.16.free_up = bf16[128,1024]{1,0:T(8,128)(2,1)S(1)} collective-permute-done((bf16[128,1024]{1,0:T(8,128)(2,1)S(1)}, bf16[128,1024]{1,0:T(8,128)(2,1)S(1)}, u32[]{:S(2)}, u32[]{:S(2)}) %collective-permute-start.16) | collective-permute-done | bytes 262176 | tf_op jit(solution)/shard_map/ppermute | solution.py:62
  137.6 5.6 %collective-permute-done.15.more_up = bf16[128,1024]{1,0:T(8,128)(2,1)S(1)} collective-permute-done((bf16[128,1024]{1,0:T(8,128)(2,1)S(1)}, bf16[128,1024]{1,0:T(8,128)(2,1)S(1)}, u32[]{:S(2)}, u32[]{:S(2)}) %collective-permute-start.15) | collective-permute-done | bytes 262176 | tf_op jit(solution)/shard_map/ppermute | solution.py:62
  143.2 4.9 %expert.1 = (bf16[128,2048]{1,0:T(8,128)(2,1)}, bf16[128,2048]{1,0:T(8,128)(2,1)}) custom-call(bf16[128,2048]{1,0:T(8,128)(2,1)S(1)} %get-tuple-element.56.rows, bf16[128,1024]{1,0:T(8,128)(2,1)S(1)} %collective-permute-done.15.more_up, bf16[128,1024]{1,0:T(8,128)(2,1)S(1)} %collective-permute-done.16.free_up, ...), custom_call_target="tpu_custom_call" | custom-call | flops 800000000 | bytes 9000000 | tf_op jit(solution)/shard_map/expert/pallas_call | solution.py:600
  (122 shorter events, 36.1 us)
Async XLA Ops:
  7.2 136.0 %all-gather.2.cloned.1.call-start = ((), (), s32[]{:S(2)}) async-start(), calls=%async_computation.2 | async-start | bytes 7077888 | tf_op jit(solution)/shard_map/all_gather | solution.py:671
  9.3 14.0 %collective-permute-start.2 = (bf16[128,2048]{1,0:T(8,128)(2,1)}, bf16[128,2048]{1,0:T(8,128)(2,1)S(1)}, u32[]{:S(2)}, u32[]{:S(2)}) collective-permute-start(bf16[128,2048]{1,0:T(8,128)(2,1)} %norm.1), channel_id=1, source_target_pairs={{0,1},{1,0},{2,3},{3,2},{4,5},{5,4},{6,7},{7,6},{8,9},{9,8},{10,11... | collective-permute-start | bytes 1572872 | tf_op jit(solution)/shard_map/ppermute | solution.py:62
  12.5 15.0 %collective-permute-start = (bf16[128,2048]{1,0:T(8,128)(2,1)}, bf16[128,2048]{1,0:T(8,128)(2,1)S(1)}, u32[]{:S(2)}, u32[]{:S(2)}) collective-permute-start(bf16[128,2048]{1,0:T(8,128)(2,1)} %norm.1), channel_id=1, source_target_pairs={{0,2},{2,4},{4,6},{6,0},{1,3},{3,5},{5,7},{7,1},{8,10},{10,12},{12... | collective-permute-start | bytes 1572872 | tf_op jit(solution)/shard_map/ppermute | solution.py:62
  12.5 15.0 %collective-permute-start.1 = (bf16[128,2048]{1,0:T(8,128)(2,1)}, bf16[128,2048]{1,0:T(8,128)(2,1)S(1)}, u32[]{:S(2)}, u32[]{:S(2)}) collective-permute-start(bf16[128,2048]{1,0:T(8,128)(2,1)} %norm.1), channel_id=1, source_target_pairs={{0,6},{2,0},{4,2},{6,4},{1,7},{3,1},{5,3},{7,5},{8,14},{10,8},{12,... | collective-permute-start | bytes 1572872 | tf_op jit(solution)/shard_map/ppermute | solution.py:62
  27.5 3.7 %collective-permute-start.5 = (bf16[128,2048]{1,0:T(8,128)(2,1)S(1)}, bf16[128,2048]{1,0:T(8,128)(2,1)S(1)}, u32[]{:S(2)}, u32[]{:S(2)}) collective-permute-start(bf16[128,2048]{1,0:T(8,128)(2,1)S(1)} %collective-permute-done.1), channel_id=1, source_target_pairs={{0,1},{1,0},{2,3},{3,2},{4,5},{5,4},{6,7},{7,6},{8,9},{9,8},{10,11... | collective-permute-start | bytes 1572872 | tf_op jit(solution)/shard_map/ppermute | solution.py:62
  28.3 2.9 %collective-permute-start.6 = (bf16[128,2048]{1,0:T(8,128)(2,1)S(1)}, bf16[128,2048]{1,0:T(8,128)(2,1)S(1)}, u32[]{:S(2)}, u32[]{:S(2)}) collective-permute-start(bf16[128,2048]{1,0:T(8,128)(2,1)S(1)} %collective-permute-done), channel_id=1, source_target_pairs={{0,1},{1,0},{2,3},{3,2},{4,5},{5,4},{6,7},{7,6},{8,9},{9,8},{10,11... | collective-permute-start | bytes 1572872 | tf_op jit(solution)/shard_map/ppermute | solution.py:62
  28.3 8.7 %collective-permute-start.3 = (bf16[64,2048]{1,0:T(8,128)(2,1)S(1)}, bf16[64,2048]{1,0:T(8,128)(2,1)S(1)}, u32[]{:S(2)}, u32[]{:S(2)}) collective-permute-start(bf16[64,2048]{1,0:T(8,128)(2,1)S(1)} %slice.47), channel_id=1, source_target_pairs={{0,2},{2,4},{4,6},{6,0},{1,3},{3,5},{5,7},{7,1},{8,10},{10,12},{12... | collective-permute-start | bytes 786440 | tf_op jit(solution)/shard_map/ppermute | solution.py:62
  28.4 8.6 %collective-permute-start.4 = (bf16[64,2048]{1,0:T(8,128)(2,1)S(1)}, bf16[64,2048]{1,0:T(8,128)(2,1)S(1)}, u32[]{:S(2)}, u32[]{:S(2)}) collective-permute-start(bf16[64,2048]{1,0:T(8,128)(2,1)S(1)} %slice.48), channel_id=1, source_target_pairs={{0,6},{2,0},{4,2},{6,4},{1,7},{3,1},{5,3},{7,5},{8,14},{10,8},{12,... | collective-permute-start | bytes 786440 | tf_op jit(solution)/shard_map/ppermute | solution.py:62
  37.1 3.2 %collective-permute-start.7 = (bf16[128,2048]{1,0:T(8,128)(2,1)S(1)}, bf16[128,2048]{1,0:T(8,128)(2,1)S(1)}, u32[]{:S(2)}, u32[]{:S(2)}) collective-permute-start(bf16[128,2048]{1,0:T(8,128)(2,1)S(1)} %pad_maximum_fusion.6), channel_id=1, source_target_pairs={{0,1},{1,0},{2,3},{3,2},{4,5},{5,4},{6,7},{7,6},{8,9},{9,8},{10,11... | collective-permute-start | bytes 1572872 | tf_op jit(solution)/shard_map/ppermute | solution.py:62
  45.2 3.8 %collective-permute-start.8 = (bf16[16,1024]{1,0:T(8,128)(2,1)S(1)}, bf16[16,1024]{1,0:T(8,128)(2,1)S(1)}, u32[]{:S(2)}, u32[]{:S(2)}) collective-permute-start(bf16[16,1024]{1,0:T(8,128)(2,1)S(1)} %select_select_fusion), channel_id=1, source_target_pairs={{0,8},{8,16},{16,24},{24,32},{32,40},{40,48},{48,56},{56,64},{64,7... | collective-permute-start | bytes 98312 | tf_op jit(solution)/shard_map/ppermute | solution.py:66
  65.7 9.7 %all-to-all-start = ((bf16[4,128,256]{2,1,0:T(8,128)(2,1)}), bf16[4,128,256]{2,1,0:T(8,128)(2,1)S(1)}, u32[]{:S(2)}, u32[]{:S(2)}) async-start(bf16[4,128,256]{2,1,0:T(8,128)(2,1)} %get-tuple-element.50), calls=%async_computation | async-start | bytes 524288 | tf_op jit(solution)/shard_map/all_to_all | solution.py:706
  69.8 25.6 %copy-start.28 = (bf16[128]{0:T(256)(128)(2,1)S(1)}, bf16[128]{0:T(256)(128)(2,1)}, u32[]{:S(2)}) copy-start(bf16[128]{0:T(256)(128)(2,1)} %param.27) | copy-start | bytes 772
  78.2 18.6 %collective-permute-start.9 = (bf16[128,256]{1,0:T(8,128)(2,1)}, bf16[128,256]{1,0:T(8,128)(2,1)S(1)}, u32[]{:S(2)}, u32[]{:S(2)}) collective-permute-start(bf16[128,256]{1,0:T(8,128)(2,1)} %get-tuple-element.52), channel_id=1, source_target_pairs={{0,32},{32,64},{64,96},{96,128},{128,160},{160,192},{192,224},{1,3... | collective-permute-start | bytes 196616 | tf_op jit(solution)/shard_map/ppermute | solution.py:66
  82.5 14.3 %collective-permute-start.10 = (bf16[128,256]{1,0:T(8,128)(2,1)}, bf16[128,256]{1,0:T(8,128)(2,1)S(1)}, u32[]{:S(2)}, u32[]{:S(2)}) collective-permute-start(bf16[128,256]{1,0:T(8,128)(2,1)} %get-tuple-element.52), channel_id=1, source_target_pairs={{0,64},{32,96},{64,128},{96,160},{128,192},{160,224},{1,65},{33,97... | collective-permute-start | bytes 196616 | tf_op jit(solution)/shard_map/ppermute | solution.py:66
  87.8 9.0 %collective-permute-start.11 = (bf16[128,256]{1,0:T(8,128)(2,1)}, bf16[128,256]{1,0:T(8,128)(2,1)S(1)}, u32[]{:S(2)}, u32[]{:S(2)}) collective-permute-start(bf16[128,256]{1,0:T(8,128)(2,1)} %get-tuple-element.52), channel_id=1, source_target_pairs={{0,96},{32,128},{64,160},{96,192},{128,224},{1,97},{33,129},{65,16... | collective-permute-start | bytes 196616 | tf_op jit(solution)/shard_map/ppermute | solution.py:66
  93.1 3.6 %collective-permute-start.12 = (bf16[128,128]{1,0:T(8,128)(2,1)}, bf16[128,128]{1,0:T(8,128)(2,1)S(1)}, u32[]{:S(2)}, u32[]{:S(2)}) collective-permute-start(bf16[128,128]{1,0:T(8,128)(2,1)} %get-tuple-element.53), channel_id=1, source_target_pairs={{0,128},{32,160},{64,192},{96,224},{1,129},{33,161},{65,193},{97,2... | collective-permute-start | bytes 98312 | tf_op jit(solution)/shard_map/ppermute | solution.py:66
  99.8 11.2 %all-to-all-start.1 = ((bf16[4,128,128]{2,1,0:T(8,128)(2,1)}), bf16[4,128,128]{2,1,0:T(8,128)(2,1)S(1)}, u32[]{:S(2)}, u32[]{:S(2)}) async-start(bf16[4,128,128]{2,1,0:T(8,128)(2,1)} %open.1), calls=%async_computation.1 | async-start | bytes 262144 | tf_op jit(solution)/shard_map/all_to_all | solution.py:712
  114.3 8.3 %collective-permute-start.13 = (bf16[4,128,2048]{2,1,0:T(8,128)(2,1)S(1)}, bf16[4,128,2048]{2,1,0:T(8,128)(2,1)S(1)}, u32[]{:S(2)}, u32[]{:S(2)}) collective-permute-start(bf16[4,128,2048]{2,1,0:T(8,128)(2,1)S(1)} %out.3), channel_id=1, source_target_pairs={{0,1},{1,0},{2,3},{3,2},{4,5},{5,4},{6,7},{7,6},{8,9},{9,8},{10,11... | collective-permute-start | bytes 6291464 | tf_op jit(solution)/shard_map/ppermute | solution.py:62
  123.0 8.9 %collective-permute-start.14 = (bf16[128,1024]{1,0:T(8,128)(2,1)S(1)}, bf16[128,1024]{1,0:T(8,128)(2,1)S(1)}, u32[]{:S(2)}, u32[]{:S(2)}) collective-permute-start(bf16[128,1024]{1,0:T(8,128)(2,1)S(1)} %get-tuple-element.58), channel_id=1, source_target_pairs={{0,2},{2,4},{4,6},{6,0},{1,3},{3,5},{5,7},{7,1},{8,10},{10,12},{12... | collective-permute-start | bytes 786440 | tf_op jit(solution)/shard_map/ppermute | solution.py:62
  124.1 8.0 %collective-permute-start.18 = (bf16[128,1024]{1,0:T(8,128)(2,1)S(1)}, bf16[128,1024]{1,0:T(8,128)(2,1)S(1)}, u32[]{:S(2)}, u32[]{:S(2)}) collective-permute-start(bf16[128,1024]{1,0:T(8,128)(2,1)S(1)} %get-tuple-element.62), channel_id=1, source_target_pairs={{0,6},{2,0},{4,2},{6,4},{1,7},{3,1},{5,3},{7,5},{8,14},{10,8},{12,... | collective-permute-start | bytes 786440 | tf_op jit(solution)/shard_map/ppermute | solution.py:62
  125.9 11.6 %collective-permute-start.16 = (bf16[128,1024]{1,0:T(8,128)(2,1)S(1)}, bf16[128,1024]{1,0:T(8,128)(2,1)S(1)}, u32[]{:S(2)}, u32[]{:S(2)}) collective-permute-start(bf16[128,1024]{1,0:T(8,128)(2,1)S(1)} %get-tuple-element.59), channel_id=1, source_target_pairs={{0,2},{2,4},{4,6},{6,0},{1,3},{3,5},{5,7},{7,1},{8,10},{10,12},{12... | collective-permute-start | bytes 786440 | tf_op jit(solution)/shard_map/ppermute | solution.py:62
  125.9 11.6 %collective-permute-start.17 = (bf16[128,1024]{1,0:T(8,128)(2,1)S(1)}, bf16[128,1024]{1,0:T(8,128)(2,1)S(1)}, u32[]{:S(2)}, u32[]{:S(2)}) collective-permute-start(bf16[128,1024]{1,0:T(8,128)(2,1)S(1)} %get-tuple-element.60), channel_id=1, source_target_pairs={{0,6},{2,0},{4,2},{6,4},{1,7},{3,1},{5,3},{7,5},{8,14},{10,8},{12,... | collective-permute-start | bytes 786440 | tf_op jit(solution)/shard_map/ppermute | solution.py:62
  132.0 11.2 %collective-permute-start.15 = (bf16[128,1024]{1,0:T(8,128)(2,1)S(1)}, bf16[128,1024]{1,0:T(8,128)(2,1)S(1)}, u32[]{:S(2)}, u32[]{:S(2)}) collective-permute-start(bf16[128,1024]{1,0:T(8,128)(2,1)S(1)} %add_convert_fusion.1), channel_id=1, source_target_pairs={{0,2},{2,4},{4,6},{6,0},{1,3},{3,5},{5,7},{7,1},{8,10},{10,12},{12... | collective-permute-start | bytes 786440 | tf_op jit(solution)/shard_map/ppermute | solution.py:62
  132.2 11.0 %collective-permute-start.19 = (bf16[128,1024]{1,0:T(8,128)(2,1)S(1)}, bf16[128,1024]{1,0:T(8,128)(2,1)S(1)}, u32[]{:S(2)}, u32[]{:S(2)}) collective-permute-start(bf16[128,1024]{1,0:T(8,128)(2,1)S(1)} %add_convert_fusion), channel_id=1, source_target_pairs={{0,6},{2,0},{4,2},{6,4},{1,7},{3,1},{5,3},{7,5},{8,14},{10,8},{12,... | collective-permute-start | bytes 786440 | tf_op jit(solution)/shard_map/ppermute | solution.py:62
  (28 other events, 236.5 us)
Sparse Core Ops, SparseCore 0:
  43.6 44.7 all-gather.1
where the time goes:
time: 156 us; the launch traced here: 155 us
  starting transfers between devices  50.4 us (32%)
  Pallas kernels  43 us (28%)
  waiting for transfers between devices  20.8 us (13%)
  between operations  14.6 us (9%)
  matrix products  13.6 us (9%)
  local copies, waits for them, and re-layouts  11.1 us (7%)
    ppermute x15, starting transfers between devices, turn(): lax.ppermute(value, axis, [(i, (i + steps) % count) for i in range(count)])  24 us
    ppermute x5, starting transfers between devices, push(): lax.ppermute(value, axis, [(i, i + steps) for i in range(count - steps)])  18.9 us
    ppermute x15, waiting for transfers between devices, turn(): lax.ppermute(value, axis, [(i, (i + steps) % count) for i in range(count)])  17.7 us
    pallas_call x1, Pallas kernels, state_call(): pl.pallas_call(state_kernel, out_shape=(jax.ShapeDtypeStruct((HEADS, DK,...  16.7 us
    unnamed x65, local copies, waits for them, and re-layouts  9.93 us
    pallas_call x1, Pallas kernels, read_call(): pl.pallas_call(read_kernel, out_shape=pltpu.HBM((NC, NY, HEADS, ROWS, 2 *...  7.86 us
    dot_general x3, matrix products, project(): return jnp.dot(rows, weight, preferred_element_type=F32).astype(BF16)  7.76 us
    pallas_call x2, Pallas kernels, out_call(): pl.pallas_call(lambda *refs: out_kernel(other, *refs), grid=(NY // 2,), o...  6.56 us
  transfers between devices with their start and end apart: 23, of which 9 were waited for; matrix products, arithmetic and copies ran while one was open for 12% of the time, Pallas kernels for 23%

commit v1 on v0

--- a/solution.py
+++ b/solution.py
@@ -336,11 +336,12 @@
 
 
 def read_kernel(
-    scal, piece_a, piece_b, piece_c, tail, taps, xs, vs, khat, logs, out, raw, sems
+    half, scal, piece_a, piece_b, piece_c, tail, taps, xs, vs, khat, logs, *rest
 ):
-    step = pl.program_id(0)
-
-    @pl.when(step == 0)
+    out, raw, sems = rest[-3:]
+    step = pl.program_id(0) + half * CHUNKS // NC // 2
+
+    @pl.when(pl.program_id(0) == 0)
     def _():
         raw[0:LEAD, :] = tail[...]
         fetch_rows(scal, (piece_a, piece_b, piece_c), raw, sems, 0, COL_K, 0)
@@ -374,38 +375,41 @@
             out[other, head] = (found + dot(scores, vs[core, head])).astype(BF16)
 
 
-def read_call(scal, pieces, tail, taps, xs, vs, khat, logs):
+def read_call(half, scal, pieces, tail, taps, xs, vs, khat, logs, *found):
     hbm = pl.BlockSpec(memory_space=pltpu.HBM)
+    skip = half * CHUNKS // NC // 2
     return pl.pallas_call(
-        read_kernel,
+        lambda *refs: read_kernel(half, *refs),
         out_shape=pltpu.HBM((NC, NY, HEADS, ROWS, 2 * DK), BF16),
         grid_spec=pltpu.PrefetchScalarGridSpec(
             num_scalar_prefetch=1,
-            grid=(CHUNKS // NC,),
+            grid=(CHUNKS // NC // 2,),
             in_specs=[
                 hbm,
                 hbm,
                 hbm,
                 pl.BlockSpec((LEAD, COL_K), lambda c, scal: (0, 0)),
                 pl.BlockSpec((4, COL_K), lambda c, scal: (0, 0)),
-                pl.BlockSpec((NC, KEYS, DK, 4 * DK), lambda c, scal: (c, 0, 0, 0)),
-                pl.BlockSpec((NC, HEADS, ROWS, 2 * DK), lambda c, scal: (c, 0, 0, 0)),
-                pl.BlockSpec((NC, KEYS, ROWS, DK), lambda c, scal: (c, 0, 0, 0)),
-                pl.BlockSpec((NC, ROWS, 128), lambda c, scal: (c, 0, 0)),
-            ],
+                pl.BlockSpec((NC, KEYS, DK, 4 * DK), lambda c, scal: (c + skip, 0, 0, 0)),
+                pl.BlockSpec((NC, HEADS, ROWS, 2 * DK), lambda c, scal: (c + skip, 0, 0, 0)),
+                pl.BlockSpec((NC, KEYS, ROWS, DK), lambda c, scal: (c + skip, 0, 0, 0)),
+                pl.BlockSpec((NC, ROWS, 128), lambda c, scal: (c + skip, 0, 0)),
+            ]
+            + [hbm] * len(found),
             out_specs=pl.BlockSpec(
                 (NC, None, HEADS, ROWS, 2 * DK),
-                lambda c, scal: (0, lax.rem(c - scal[0] + NY, NY), 0, 0, 0),
+                lambda c, scal: (0, lax.rem(c + skip - scal[0] + NY, NY), 0, 0, 0),
             ),
             scratch_shapes=[
                 pltpu.VMEM((LEAD + CHUNKS * ROWS, COL_K), BF16),
                 pltpu.SemaphoreType.DMA((CHUNKS,)),
             ],
         ),
+        input_output_aliases={10: 0} if found else {},
         compiler_params=pltpu.CompilerParams(vmem_limit_bytes=32 * MIB),
         cost_estimate=pl.CostEstimate(flops=3_000_000_000, bytes_accessed=10_000_000, transcendentals=0),
         name="read",
-    )(scal, *map(hold, pieces), tail, taps, hold(xs), hold(vs), hold(khat), hold(logs))
+    )(scal, *map(hold, pieces), tail, taps, hold(xs), hold(vs), hold(khat), hold(logs), *map(hold, found))
 
 
 def norm_kernel(tokens, gain, out):
@@ -705,13 +709,14 @@
 
     parts = lax.all_to_all(xend, "x", 0, 0, tiled=True)
     given = (tail[:, :COL_K], taps_qk[:, 0, :], xs, vs, khat, logs)
-    parts, gates_beside = lax.optimization_barrier((parts, gates_beside))
+    found = read_call(0, scal, pieces, *given)
+    parts, gates_beside, found = lax.optimization_barrier((parts, gates_beside, found))
     leads, whole, sums = row_call(parts)
     earlier = [push(whole if steps < 4 else sums, "z", steps, NZ) for steps in (1, 2, 3, 4)]
     openings = open_call(earlier, leads)
     opening = lax.all_to_all(openings, "x", 0, 0, tiled=True)
 
-    found = read_call(scal, pieces, *given)
+    found = read_call(1, scal, pieces, *given, found)
 
     gain = norm_gain.astype(F32)[None, :]
     lent = out_call(1, scal, found, gates_beside, opening, gain, w_out)

time: 156 us -> 158 us (1.013)
  waiting for transfers between devices: 20.8 us -> 17.7 us
  Pallas kernels: 43 us -> 46 us
  local copies, waits for them, and re-layouts: 11.1 us -> 13.2 us
    pallas_call x1 -> x2, Pallas kernels: 7.86 us -> 11 us  [read_call(): pl.pallas_call(lambda *refs: read_kernel(half, *refs), out_shape=pltpu.HB...]
    unnamed x65 -> x69, local copies, waits for them, and re-layouts: 9.93 us -> 12.1 us
    all_to_all x1, waiting for transfers between devices: 1.83 us -> 0.11 us  [per_device(): parts = lax.all_to_all(xend, 'x', 0, 0, tiled=True)]
    dot_general x2, matrix products: 5.79 us -> 4.2 us  [gates(): gate = jnp.dot(rows, weight_z, preferred_element_type=F32).astype(BF16)]
  transfers between devices with their start and end apart: 23 -> 23, of which waited for: 9 -> 9; matrix products, arithmetic and copies ran while one was open for 12% -> 11% of each run, Pallas kernels for 23% -> 25%
where the time goes in v1:
time: 158 us; the launch traced here: 157 us
  starting transfers between devices  50.6 us (32%)
  Pallas kernels  46 us (29%)
  waiting for transfers between devices  17.7 us (11%)
  between operations  14.6 us (9%)
  local copies, waits for them, and re-layouts  13.2 us (8%)
  matrix products  13.2 us (8%)
    ppermute x15, starting transfers between devices, turn(): lax.ppermute(value, axis, [(i, (i + steps) % count) for i in range(count)])  23.3 us
    ppermute x5, starting transfers between devices, push(): lax.ppermute(value, axis, [(i, i + steps) for i in range(count - steps)])  19.1 us
    pallas_call x1, Pallas kernels, state_call(): pl.pallas_call(state_kernel, out_shape=(jax.ShapeDtypeStruct((HEADS, DK,...  16.7 us
    ppermute x15, waiting for transfers between devices, turn(): lax.ppermute(value, axis, [(i, (i + steps) % count) for i in range(count)])  16.2 us
    unnamed x69, local copies, waits for them, and re-layouts  12.1 us
    pallas_call x2, Pallas kernels, read_call(): pl.pallas_call(lambda *refs: read_kernel(half, *refs), out_shape=pltpu.HB...  11 us
    dot_general x3, matrix products, project(): return jnp.dot(rows, weight, preferred_element_type=F32).astype(BF16)  9 us
    pallas_call x2, Pallas kernels, out_call(): pl.pallas_call(lambda *refs: out_kernel(other, *refs), grid=(NY // 2,), o...  6.57 us
  transfers between devices with their start and end apart: 23, of which 9 were waited for; matrix products, arithmetic and copies ran while one was open for 11% of the time, Pallas kernels for 25%

profile of v1, /device:TPU:1, one launch (start us, length us, event | category | flops | bytes accessed | tf_op | source)
XLA Modules:
  0.0 156.7 jit_solution(12468985756811812156)
XLA Ops:
  9.3 3.2 %collective-permute-start.2 = (bf16[128,2048]{1,0:T(8,128)(2,1)}, bf16[128,2048]{1,0:T(8,128)(2,1)S(1)}, u32[]{:S(2)}, u32[]{:S(2)}) collective-permute-start(bf16[128,2048]{1,0:T(8,128)(2,1)} %norm.1), channel_id=1, source_target_pairs={{0,1},{1,0},{2,3},{3,2},{4,5},{5,4},{6,7},{7,6},{8,9},{9,8},{10,11... | collective-permute-start | bytes 1572872 | tf_op jit(solution)/shard_map/ppermute | solution.py:62
  12.5 2.7 %collective-permute-start.1 = (bf16[128,2048]{1,0:T(8,128)(2,1)}, bf16[128,2048]{1,0:T(8,128)(2,1)S(1)}, u32[]{:S(2)}, u32[]{:S(2)}) collective-permute-start(bf16[128,2048]{1,0:T(8,128)(2,1)} %norm.1), channel_id=1, source_target_pairs={{0,6},{2,0},{4,2},{6,4},{1,7},{3,1},{5,3},{7,5},{8,14},{10,8},{12,... | collective-permute-start | bytes 1572872 | tf_op jit(solution)/shard_map/ppermute | solution.py:62
  16.3 3.6 %copy.23 = bf16[256,8,2,512]{3,1,2,0:T(8,128)(2,1)S(1)} copy(bf16[256,8,2,512]{3,2,1,0:T(2,128)(2,1)} %bitcast.25) | data formatting | bytes 8388608
  24.0 2.3 %convolution_convert_fusion.2.piece_a.refs_1_ = bf16[256,1152]{1,0:T(8,128)(2,1)} fusion(bf16[128,2048]{1,0:T(8,128)(2,1)S(1)} %collective-permute-done.2, bf16[128,2048]{1,0:T(8,128)(2,1)S(1)} %copy-done.7, bf16[2048,8]{1,0:T(8,128)(2,1)S(1)} %copy.21, bf16[2048,512]{1,0:T(8,128)(2,1)S(1)} %slice.61, bf16[2048,512]{1,0:T(8,128)(2,1)S(1)} %bitcast.27), kind=kOutput, calls=%fused_computation.7 | convolution fusion | flops 1229225984 | bytes 5865472 | tf_op jit(solution)/shard_map/dot_general | solution.py:657
  28.4 2.8 %collective-permute-start.4 = (bf16[64,2048]{1,0:T(8,128)(2,1)S(1)}, bf16[64,2048]{1,0:T(8,128)(2,1)S(1)}, u32[]{:S(2)}, u32[]{:S(2)}) collective-permute-start(bf16[64,2048]{1,0:T(8,128)(2,1)S(1)} %slice.48), channel_id=1, source_target_pairs={{0,6},{2,0},{4,2},{6,4},{1,7},{3,1},{5,3},{7,5},{8,14},{10,8},{12,... | collective-permute-start | bytes 786440 | tf_op jit(solution)/shard_map/ppermute | solution.py:62
  31.2 4.3 %convolution_convert_fusion.piece_b.refs_2_ = bf16[512,1152]{1,0:T(8,128)(2,1)S(1)} fusion(bf16[128,2048]{1,0:T(8,128)(2,1)S(1)} %collective-permute-done.6, bf16[128,2048]{1,0:T(8,128)(2,1)S(1)} %collective-permute-done.5, bf16[128,2048]{1,0:T(8,128)(2,1)S(1)} %collective-permute-done, bf16[128,2048]{1,0:T(8,128)(2,1)S(1)} %collective-permute-done.1, ...), kind=kOutput, calls=%fused_computation.3 | convolution fusion | flops 2443771904 | bytes 7503872 | tf_op jit(solution)/shard_map/dot_general | solution.py:657
  41.1 2.4 %convolution_convert_fusion.1.piece_c.refs_3_ = bf16[256,1152]{1,0:T(8,128)(2,1)} fusion(bf16[128,2048]{1,0:T(8,128)(2,1)S(1)} %collective-permute-done.7, bf16[64,2048]{1,0:T(8,128)(2,1)S(1)} %collective-permute-done.4, bf16[64,2048]{1,0:T(8,128)(2,1)S(1)} %collective-permute-done.3, bf16[2048,8]{1,0:T(8,128)(2,1)S(1)} %copy-done.10, ...), kind=kOutput, calls=%fused_computation.6 | convolution fusion | flops 1230274560 | bytes 5865472 | tf_op jit(solution)/shard_map/dot_general | solution.py:657
  52.8 16.7 %state.1 = (bf16[4,128,256]{2,1,0:T(8,128)(2,1)}, bf16[8,2,128,512]{3,2,1,0:T(8,128)(2,1)}, bf16[8,4,128,256]{3,2,1,0:T(8,128)(2,1)}, bf16[8,2,128,128]{3,2,1,0:T(8,128)(2,1)}, f32[8,128,128]{2,1,0:T(8,128)}) custom-call(s32[6]{0:T(128)S(1)} %pad_add_fusion.2.scal.refs_0_, bf16[256,1152]{1,0:T(8,128)(2,1)} %convolution_convert_fusion.2.piece_a.refs_1_, ...), custom_call_target="tpu_custom_call" | custom-call | flops 6000000000 | bytes 20000000 | tf_op jit(solution)/shard_map/state/pallas_call | solution.py:307
  69.5 4.1 %all-to-all-start = ((bf16[4,128,256]{2,1,0:T(8,128)(2,1)}), bf16[4,128,256]{2,1,0:T(8,128)(2,1)S(1)}, u32[]{:S(2)}, u32[]{:S(2)}) async-start(bf16[4,128,256]{2,1,0:T(8,128)(2,1)} %get-tuple-element.50), calls=%async_computation | async-start | bytes 524288 | tf_op jit(solution)/shard_map/all_to_all | solution.py:710
  73.6 5.5 %read.2.refs_10_ = bf16[2,4,4,128,256]{4,3,2,1,0:T(8,128)(2,1)} custom-call(s32[6]{0:T(128)S(1)} %pad_add_fusion.2.scal.refs_0_, bf16[256,1152]{1,0:T(8,128)(2,1)} %convolution_convert_fusion.2.piece_a.refs_1_, bf16[512,1152]{1,0:T(8,128)(2,1)} %copy-done.8, bf16[256,1152]{1,0:T(8,128)(2,1)} %convolution_convert_fusion.1.piece_c.refs_3_, ...), custom_call_target="tpu_custom_call" | custom-call | flops 3000000000 | bytes 10000000 | tf_op jit(solution)/shard_map/read/pallas_call | solution.py:381
  81.9 4.5 %collective-permute-start.9 = (bf16[128,256]{1,0:T(8,128)(2,1)}, bf16[128,256]{1,0:T(8,128)(2,1)S(1)}, u32[]{:S(2)}, u32[]{:S(2)}) collective-permute-start(bf16[128,256]{1,0:T(8,128)(2,1)} %get-tuple-element.54), channel_id=1, source_target_pairs={{0,32},{32,64},{64,96},{96,128},{128,160},{160,192},{192,224},{1,3... | collective-permute-start | bytes 196616 | tf_op jit(solution)/shard_map/ppermute | solution.py:66
  86.4 5.3 %collective-permute-start.10 = (bf16[128,256]{1,0:T(8,128)(2,1)}, bf16[128,256]{1,0:T(8,128)(2,1)S(1)}, u32[]{:S(2)}, u32[]{:S(2)}) collective-permute-start(bf16[128,256]{1,0:T(8,128)(2,1)} %get-tuple-element.54), channel_id=1, source_target_pairs={{0,64},{32,96},{64,128},{96,160},{128,192},{160,224},{1,65},{33,97... | collective-permute-start | bytes 196616 | tf_op jit(solution)/shard_map/ppermute | solution.py:66
  91.8 5.4 %collective-permute-start.11 = (bf16[128,256]{1,0:T(8,128)(2,1)}, bf16[128,256]{1,0:T(8,128)(2,1)S(1)}, u32[]{:S(2)}, u32[]{:S(2)}) collective-permute-start(bf16[128,256]{1,0:T(8,128)(2,1)} %get-tuple-element.54), channel_id=1, source_target_pairs={{0,96},{32,128},{64,160},{96,192},{128,224},{1,97},{33,129},{65,16... | collective-permute-start | bytes 196616 | tf_op jit(solution)/shard_map/ppermute | solution.py:66
  103.8 4.2 %all-to-all-start.1 = ((bf16[4,128,128]{2,1,0:T(8,128)(2,1)}), bf16[4,128,128]{2,1,0:T(8,128)(2,1)S(1)}, u32[]{:S(2)}, u32[]{:S(2)}) async-start(bf16[4,128,128]{2,1,0:T(8,128)(2,1)} %open.1), calls=%async_computation.1 | async-start | bytes 262144 | tf_op jit(solution)/shard_map/all_to_all | solution.py:717
  108.0 5.5 %read.3.refs_1_ = bf16[2,4,4,128,256]{4,3,2,1,0:T(8,128)(2,1)} custom-call(s32[6]{0:T(128)S(1)} %pad_add_fusion.2.scal.refs_0_, bf16[256,1152]{1,0:T(8,128)(2,1)} %convolution_convert_fusion.2.piece_a.refs_1_, bf16[512,1152]{1,0:T(8,128)(2,1)} %copy-done.8, ...), custom_call_target="tpu_custom_call", output_to_operand_aliasing={{}: (10, {})} | custom-call | flops 3000000000 | bytes 10000000 | tf_op jit(solution)/shard_map/read/pallas_call | solution.py:381
  113.5 3.3 %out.3 = bf16[4,128,2048]{2,1,0:T(8,128)(2,1)S(1)} custom-call(s32[6]{0:T(128)S(1)} %pad_add_fusion.2.scal.refs_0_, bf16[2,4,4,128,256]{4,3,2,1,0:T(8,128)(2,1)} %read.3.refs_1_, bf16[4,128,512]{2,1,0:T(8,128)(2,1)} %bitcast.31, bf16[4,128,128]{2,1,0:T(8,128)(2,1)S(1)} %all-to-all-done.1.refs_3_, f32[1,128]{1,0:T(1,128)S(1)} %bitcast_convert_fusion.refs_4_, ...), custom_call_target="tpu_custom_call" | custom-call | flops 1200000000 | bytes 6000000 | tf_op jit(solution)/shard_map/out/pallas_call | solution.py:514
  116.8 3.8 %collective-permute-start.13 = (bf16[4,128,2048]{2,1,0:T(8,128)(2,1)S(1)}, bf16[4,128,2048]{2,1,0:T(8,128)(2,1)S(1)}, u32[]{:S(2)}, u32[]{:S(2)}) collective-permute-start(bf16[4,128,2048]{2,1,0:T(8,128)(2,1)S(1)} %out.3), channel_id=1, source_target_pairs={{0,1},{1,0},{2,3},{3,2},{4,5},{5,4},{6,7},{7,6},{8,9},{9,8},{10,11... | collective-permute-start | bytes 6291464 | tf_op jit(solution)/shard_map/ppermute | solution.py:62
  120.6 3.3 %out.2.own = bf16[4,128,2048]{2,1,0:T(8,128)(2,1)S(1)} custom-call(s32[6]{0:T(128)S(1)} %pad_add_fusion.2.scal.refs_0_, bf16[2,4,4,128,256]{4,3,2,1,0:T(8,128)(2,1)} %read.3.refs_1_, bf16[4,128,512]{2,1,0:T(8,128)(2,1)} %bitcast.30, bf16[4,128,128]{2,1,0:T(8,128)(2,1)S(1)} %all-to-all-done.1.refs_3_, f32[1,128]{1,0:T(1,128)S(1)} %bitcast_convert_fusion.refs_4_, ...), custom_call_target="tpu_custom_call" | custom-call | flops 1200000000 | bytes 6000000 | tf_op jit(solution)/shard_map/out/pallas_call | solution.py:514
  127.7 2.7 %collective-permute-start.17 = (bf16[128,1024]{1,0:T(8,128)(2,1)S(1)}, bf16[128,1024]{1,0:T(8,128)(2,1)S(1)}, u32[]{:S(2)}, u32[]{:S(2)}) collective-permute-start(bf16[128,1024]{1,0:T(8,128)(2,1)S(1)} %get-tuple-element.62), channel_id=1, source_target_pairs={{0,6},{2,0},{4,2},{6,4},{1,7},{3,1},{5,3},{7,5},{8,14},{10,8},{12,... | collective-permute-start | bytes 786440 | tf_op jit(solution)/shard_map/ppermute | solution.py:62
  130.3 3.3 %collective-permute-done.14 = bf16[128,1024]{1,0:T(8,128)(2,1)S(1)} collective-permute-done((bf16[128,1024]{1,0:T(8,128)(2,1)S(1)}, bf16[128,1024]{1,0:T(8,128)(2,1)S(1)}, u32[]{:S(2)}, u32[]{:S(2)}) %collective-permute-start.14) | collective-permute-done | bytes 262176 | tf_op jit(solution)/shard_map/ppermute | solution.py:62
  133.9 2.7 %collective-permute-start.19 = (bf16[128,1024]{1,0:T(8,128)(2,1)S(1)}, bf16[128,1024]{1,0:T(8,128)(2,1)S(1)}, u32[]{:S(2)}, u32[]{:S(2)}) collective-permute-start(bf16[128,1024]{1,0:T(8,128)(2,1)S(1)} %add_convert_fusion), channel_id=1, source_target_pairs={{0,6},{2,0},{4,2},{6,4},{1,7},{3,1},{5,3},{7,5},{8,14},{10,8},{12,... | collective-permute-start | bytes 786440 | tf_op jit(solution)/shard_map/ppermute | solution.py:62
  136.7 2.6 %collective-permute-done.16.free_up = bf16[128,1024]{1,0:T(8,128)(2,1)S(1)} collective-permute-done((bf16[128,1024]{1,0:T(8,128)(2,1)S(1)}, bf16[128,1024]{1,0:T(8,128)(2,1)S(1)}, u32[]{:S(2)}, u32[]{:S(2)}) %collective-permute-start.16) | collective-permute-done | bytes 262176 | tf_op jit(solution)/shard_map/ppermute | solution.py:62
  139.3 5.6 %collective-permute-done.15.more_up = bf16[128,1024]{1,0:T(8,128)(2,1)S(1)} collective-permute-done((bf16[128,1024]{1,0:T(8,128)(2,1)S(1)}, bf16[128,1024]{1,0:T(8,128)(2,1)S(1)}, u32[]{:S(2)}, u32[]{:S(2)}) %collective-permute-start.15) | collective-permute-done | bytes 262176 | tf_op jit(solution)/shard_map/ppermute | solution.py:62
  145.0 4.9 %expert.1 = (bf16[128,2048]{1,0:T(8,128)(2,1)}, bf16[128,2048]{1,0:T(8,128)(2,1)}) custom-call(bf16[128,2048]{1,0:T(8,128)(2,1)S(1)} %get-tuple-element.58.rows, bf16[128,1024]{1,0:T(8,128)(2,1)S(1)} %collective-permute-done.15.more_up, bf16[128,1024]{1,0:T(8,128)(2,1)S(1)} %collective-permute-done.16.free_up, ...), custom_call_target="tpu_custom_call" | custom-call | flops 800000000 | bytes 9000000 | tf_op jit(solution)/shard_map/expert/pallas_call | solution.py:604
  (127 shorter events, 37.4 us)
Async XLA Ops:
  7.2 137.8 %all-gather.2.cloned.1.call-start = ((), (), s32[]{:S(2)}) async-start(), calls=%async_computation.2 | async-start | bytes 7077888 | tf_op jit(solution)/shard_map/all_gather | solution.py:675
  9.3 14.2 %collective-permute-start.2 = (bf16[128,2048]{1,0:T(8,128)(2,1)}, bf16[128,2048]{1,0:T(8,128)(2,1)S(1)}, u32[]{:S(2)}, u32[]{:S(2)}) collective-permute-start(bf16[128,2048]{1,0:T(8,128)(2,1)} %norm.1), channel_id=1, source_target_pairs={{0,1},{1,0},{2,3},{3,2},{4,5},{5,4},{6,7},{7,6},{8,9},{9,8},{10,11... | collective-permute-start | bytes 1572872 | tf_op jit(solution)/shard_map/ppermute | solution.py:62
  12.5 15.0 %collective-permute-start = (bf16[128,2048]{1,0:T(8,128)(2,1)}, bf16[128,2048]{1,0:T(8,128)(2,1)S(1)}, u32[]{:S(2)}, u32[]{:S(2)}) collective-permute-start(bf16[128,2048]{1,0:T(8,128)(2,1)} %norm.1), channel_id=1, source_target_pairs={{0,2},{2,4},{4,6},{6,0},{1,3},{3,5},{5,7},{7,1},{8,10},{10,12},{12... | collective-permute-start | bytes 1572872 | tf_op jit(solution)/shard_map/ppermute | solution.py:62
  12.5 15.0 %collective-permute-start.1 = (bf16[128,2048]{1,0:T(8,128)(2,1)}, bf16[128,2048]{1,0:T(8,128)(2,1)S(1)}, u32[]{:S(2)}, u32[]{:S(2)}) collective-permute-start(bf16[128,2048]{1,0:T(8,128)(2,1)} %norm.1), channel_id=1, source_target_pairs={{0,6},{2,0},{4,2},{6,4},{1,7},{3,1},{5,3},{7,5},{8,14},{10,8},{12,... | collective-permute-start | bytes 1572872 | tf_op jit(solution)/shard_map/ppermute | solution.py:62
  27.5 3.7 %collective-permute-start.5 = (bf16[128,2048]{1,0:T(8,128)(2,1)S(1)}, bf16[128,2048]{1,0:T(8,128)(2,1)S(1)}, u32[]{:S(2)}, u32[]{:S(2)}) collective-permute-start(bf16[128,2048]{1,0:T(8,128)(2,1)S(1)} %collective-permute-done.1), channel_id=1, source_target_pairs={{0,1},{1,0},{2,3},{3,2},{4,5},{5,4},{6,7},{7,6},{8,9},{9,8},{10,11... | collective-permute-start | bytes 1572872 | tf_op jit(solution)/shard_map/ppermute | solution.py:62
  28.3 2.9 %collective-permute-start.6 = (bf16[128,2048]{1,0:T(8,128)(2,1)S(1)}, bf16[128,2048]{1,0:T(8,128)(2,1)S(1)}, u32[]{:S(2)}, u32[]{:S(2)}) collective-permute-start(bf16[128,2048]{1,0:T(8,128)(2,1)S(1)} %collective-permute-done), channel_id=1, source_target_pairs={{0,1},{1,0},{2,3},{3,2},{4,5},{5,4},{6,7},{7,6},{8,9},{9,8},{10,11... | collective-permute-start | bytes 1572872 | tf_op jit(solution)/shard_map/ppermute | solution.py:62
  28.4 8.7 %collective-permute-start.3 = (bf16[64,2048]{1,0:T(8,128)(2,1)S(1)}, bf16[64,2048]{1,0:T(8,128)(2,1)S(1)}, u32[]{:S(2)}, u32[]{:S(2)}) collective-permute-start(bf16[64,2048]{1,0:T(8,128)(2,1)S(1)} %slice.47), channel_id=1, source_target_pairs={{0,2},{2,4},{4,6},{6,0},{1,3},{3,5},{5,7},{7,1},{8,10},{10,12},{12... | collective-permute-start | bytes 786440 | tf_op jit(solution)/shard_map/ppermute | solution.py:62
  28.4 8.6 %collective-permute-start.4 = (bf16[64,2048]{1,0:T(8,128)(2,1)S(1)}, bf16[64,2048]{1,0:T(8,128)(2,1)S(1)}, u32[]{:S(2)}, u32[]{:S(2)}) collective-permute-start(bf16[64,2048]{1,0:T(8,128)(2,1)S(1)} %slice.48), channel_id=1, source_target_pairs={{0,6},{2,0},{4,2},{6,4},{1,7},{3,1},{5,3},{7,5},{8,14},{10,8},{12,... | collective-permute-start | bytes 786440 | tf_op jit(solution)/shard_map/ppermute | solution.py:62
  37.1 3.2 %collective-permute-start.7 = (bf16[128,2048]{1,0:T(8,128)(2,1)S(1)}, bf16[128,2048]{1,0:T(8,128)(2,1)S(1)}, u32[]{:S(2)}, u32[]{:S(2)}) collective-permute-start(bf16[128,2048]{1,0:T(8,128)(2,1)S(1)} %pad_maximum_fusion.6), channel_id=1, source_target_pairs={{0,1},{1,0},{2,3},{3,2},{4,5},{5,4},{6,7},{7,6},{8,9},{9,8},{10,11... | collective-permute-start | bytes 1572872 | tf_op jit(solution)/shard_map/ppermute | solution.py:62
  49.1 3.7 %collective-permute-start.8 = (bf16[16,1024]{1,0:T(8,128)(2,1)S(1)}, bf16[16,1024]{1,0:T(8,128)(2,1)S(1)}, u32[]{:S(2)}, u32[]{:S(2)}) collective-permute-start(bf16[16,1024]{1,0:T(8,128)(2,1)S(1)} %select_select_fusion), channel_id=1, source_target_pairs={{0,8},{8,16},{16,24},{24,32},{32,40},{40,48},{48,56},{56,64},{64,7... | collective-permute-start | bytes 98312 | tf_op jit(solution)/shard_map/ppermute | solution.py:66
  69.5 9.7 %all-to-all-start = ((bf16[4,128,256]{2,1,0:T(8,128)(2,1)}), bf16[4,128,256]{2,1,0:T(8,128)(2,1)S(1)}, u32[]{:S(2)}, u32[]{:S(2)}) async-start(bf16[4,128,256]{2,1,0:T(8,128)(2,1)} %get-tuple-element.50), calls=%async_computation | async-start | bytes 524288 | tf_op jit(solution)/shard_map/all_to_all | solution.py:710
  73.6 25.9 %copy-start.30 = (bf16[128]{0:T(256)(128)(2,1)S(1)}, bf16[128]{0:T(256)(128)(2,1)}, u32[]{:S(2)}) copy-start(bf16[128]{0:T(256)(128)(2,1)} %param.27) | copy-start | bytes 772
  81.9 18.9 %collective-permute-start.9 = (bf16[128,256]{1,0:T(8,128)(2,1)}, bf16[128,256]{1,0:T(8,128)(2,1)S(1)}, u32[]{:S(2)}, u32[]{:S(2)}) collective-permute-start(bf16[128,256]{1,0:T(8,128)(2,1)} %get-tuple-element.54), channel_id=1, source_target_pairs={{0,32},{32,64},{64,96},{96,128},{128,160},{160,192},{192,224},{1,3... | collective-permute-start | bytes 196616 | tf_op jit(solution)/shard_map/ppermute | solution.py:66
  86.4 14.4 %collective-permute-start.10 = (bf16[128,256]{1,0:T(8,128)(2,1)}, bf16[128,256]{1,0:T(8,128)(2,1)S(1)}, u32[]{:S(2)}, u32[]{:S(2)}) collective-permute-start(bf16[128,256]{1,0:T(8,128)(2,1)} %get-tuple-element.54), channel_id=1, source_target_pairs={{0,64},{32,96},{64,128},{96,160},{128,192},{160,224},{1,65},{33,97... | collective-permute-start | bytes 196616 | tf_op jit(solution)/shard_map/ppermute | solution.py:66
  91.8 9.0 %collective-permute-start.11 = (bf16[128,256]{1,0:T(8,128)(2,1)}, bf16[128,256]{1,0:T(8,128)(2,1)S(1)}, u32[]{:S(2)}, u32[]{:S(2)}) collective-permute-start(bf16[128,256]{1,0:T(8,128)(2,1)} %get-tuple-element.54), channel_id=1, source_target_pairs={{0,96},{32,128},{64,160},{96,192},{128,224},{1,97},{33,129},{65,16... | collective-permute-start | bytes 196616 | tf_op jit(solution)/shard_map/ppermute | solution.py:66
  97.2 3.6 %collective-permute-start.12 = (bf16[128,128]{1,0:T(8,128)(2,1)}, bf16[128,128]{1,0:T(8,128)(2,1)S(1)}, u32[]{:S(2)}, u32[]{:S(2)}) collective-permute-start(bf16[128,128]{1,0:T(8,128)(2,1)} %get-tuple-element.55), channel_id=1, source_target_pairs={{0,128},{32,160},{64,192},{96,224},{1,129},{33,161},{65,193},{97,2... | collective-permute-start | bytes 98312 | tf_op jit(solution)/shard_map/ppermute | solution.py:66
  103.8 9.7 %all-to-all-start.1 = ((bf16[4,128,128]{2,1,0:T(8,128)(2,1)}), bf16[4,128,128]{2,1,0:T(8,128)(2,1)S(1)}, u32[]{:S(2)}, u32[]{:S(2)}) async-start(bf16[4,128,128]{2,1,0:T(8,128)(2,1)} %open.1), calls=%async_computation.1 | async-start | bytes 262144 | tf_op jit(solution)/shard_map/all_to_all | solution.py:717
  116.8 7.6 %collective-permute-start.13 = (bf16[4,128,2048]{2,1,0:T(8,128)(2,1)S(1)}, bf16[4,128,2048]{2,1,0:T(8,128)(2,1)S(1)}, u32[]{:S(2)}, u32[]{:S(2)}) collective-permute-start(bf16[4,128,2048]{2,1,0:T(8,128)(2,1)S(1)} %out.3), channel_id=1, source_target_pairs={{0,1},{1,0},{2,3},{3,2},{4,5},{5,4},{6,7},{7,6},{8,9},{9,8},{10,11... | collective-permute-start | bytes 6291464 | tf_op jit(solution)/shard_map/ppermute | solution.py:62
  124.9 8.8 %collective-permute-start.14 = (bf16[128,1024]{1,0:T(8,128)(2,1)S(1)}, bf16[128,1024]{1,0:T(8,128)(2,1)S(1)}, u32[]{:S(2)}, u32[]{:S(2)}) collective-permute-start(bf16[128,1024]{1,0:T(8,128)(2,1)S(1)} %get-tuple-element.60), channel_id=1, source_target_pairs={{0,2},{2,4},{4,6},{6,0},{1,3},{3,5},{5,7},{7,1},{8,10},{10,12},{12... | collective-permute-start | bytes 786440 | tf_op jit(solution)/shard_map/ppermute | solution.py:62
  126.0 7.8 %collective-permute-start.18 = (bf16[128,1024]{1,0:T(8,128)(2,1)S(1)}, bf16[128,1024]{1,0:T(8,128)(2,1)S(1)}, u32[]{:S(2)}, u32[]{:S(2)}) collective-permute-start(bf16[128,1024]{1,0:T(8,128)(2,1)S(1)} %get-tuple-element.64), channel_id=1, source_target_pairs={{0,6},{2,0},{4,2},{6,4},{1,7},{3,1},{5,3},{7,5},{8,14},{10,8},{12,... | collective-permute-start | bytes 786440 | tf_op jit(solution)/shard_map/ppermute | solution.py:62
  127.7 11.6 %collective-permute-start.16 = (bf16[128,1024]{1,0:T(8,128)(2,1)S(1)}, bf16[128,1024]{1,0:T(8,128)(2,1)S(1)}, u32[]{:S(2)}, u32[]{:S(2)}) collective-permute-start(bf16[128,1024]{1,0:T(8,128)(2,1)S(1)} %get-tuple-element.61), channel_id=1, source_target_pairs={{0,2},{2,4},{4,6},{6,0},{1,3},{3,5},{5,7},{7,1},{8,10},{10,12},{12... | collective-permute-start | bytes 786440 | tf_op jit(solution)/shard_map/ppermute | solution.py:62
  127.7 11.6 %collective-permute-start.17 = (bf16[128,1024]{1,0:T(8,128)(2,1)S(1)}, bf16[128,1024]{1,0:T(8,128)(2,1)S(1)}, u32[]{:S(2)}, u32[]{:S(2)}) collective-permute-start(bf16[128,1024]{1,0:T(8,128)(2,1)S(1)} %get-tuple-element.62), channel_id=1, source_target_pairs={{0,6},{2,0},{4,2},{6,4},{1,7},{3,1},{5,3},{7,5},{8,14},{10,8},{12,... | collective-permute-start | bytes 786440 | tf_op jit(solution)/shard_map/ppermute | solution.py:62
  133.8 11.2 %collective-permute-start.15 = (bf16[128,1024]{1,0:T(8,128)(2,1)S(1)}, bf16[128,1024]{1,0:T(8,128)(2,1)S(1)}, u32[]{:S(2)}, u32[]{:S(2)}) collective-permute-start(bf16[128,1024]{1,0:T(8,128)(2,1)S(1)} %add_convert_fusion.1), channel_id=1, source_target_pairs={{0,2},{2,4},{4,6},{6,0},{1,3},{3,5},{5,7},{7,1},{8,10},{10,12},{12... | collective-permute-start | bytes 786440 | tf_op jit(solution)/shard_map/ppermute | solution.py:62
  133.9 11.0 %collective-permute-start.19 = (bf16[128,1024]{1,0:T(8,128)(2,1)S(1)}, bf16[128,1024]{1,0:T(8,128)(2,1)S(1)}, u32[]{:S(2)}, u32[]{:S(2)}) collective-permute-start(bf16[128,1024]{1,0:T(8,128)(2,1)S(1)} %add_convert_fusion), channel_id=1, source_target_pairs={{0,6},{2,0},{4,2},{6,4},{1,7},{3,1},{5,3},{7,5},{8,14},{10,8},{12,... | collective-permute-start | bytes 786440 | tf_op jit(solution)/shard_map/ppermute | solution.py:62
  (30 other events, 183.5 us)
Sparse Core Ops, SparseCore 0:
  43.6 44.7 all-gather.1
